TPU v7x, 32 devices: a whole 2x2x4 slice. The times are simulated.
32 devices in a mesh: row: 2 (over x), col: 4 (over y, core), vir: 4 (over z).
Axes of the slice: x: 2, y: 2, z: 4, core: 2. Of those that a mesh axis runs over, the one named last changes fastest.
Arguments:
- amplitudes: bfloat16 [64, 2, 16, 4, 2, 3, 1792], P(None, 'row', None, 'col'), may hold values from -6 to 6
- integrals: bfloat16 [64, 64, 3, 1792], P('vir', 'row', None, 'col'), may hold values from -0.25 to 0.25
- hole_integrals: bfloat16 [128, 16, 4, 2, 3, 64], P(None, None, 'col'), may hold values from -0.3125 to 0.3125
- irreps: int32 [112], replicated, may hold values from 0 to 7
- occ_energy: float32 [128], replicated, may hold values from -2 to -0.5
- vir_energy: float32 [64], replicated, may hold values from 0.5 to 3
Outputs:
- increment: bfloat16 [64, 2, 16, 4, 2, 64, 64], P(None, 'row', None, 'col', None, 'vir')
All inputs are finite; a program needn't handle non-finite values.
Results may differ from a plain program's by a relative error of at most 0.001.
Values may be sent and summed in bfloat16 or wider, within the bound.
No kernel may reach another device: no remote copies, remote signals or barrier semaphores. Data moves between devices by JAX's collectives and lax.ppermute only.
A program may use at most 256 MiB of HBM per device.

v0:
```python
import jax
import jax.numpy as jnp
from jax import lax
from jax.sharding import PartitionSpec as P

NO = 128
NV = 1792
SA = 64
CW = 3
VBLK = 16


def masked_block(piece, lab_a, lab_b, lab_c, lab_d):
    left = jnp.bitwise_xor(lab_a[:, None], lab_b[None, :])
    right = jnp.bitwise_xor(lab_c[:, None], lab_d[None, :])
    keep = left[:, :, None, None] == right[None, None, :, :]
    return jnp.where(keep, piece, jnp.zeros_like(piece))


def contract(amp_rows, block):
    return lax.dot_general(
        amp_rows, block, (((1, 2), (2, 3)), ((), ())), preferred_element_type=jnp.float32
    )


def local(amplitudes, integrals, hole_integrals, irreps, occ_energy, vir_energy):
    vir_pos = lax.axis_index("vir")
    row_pos = lax.axis_index("row")
    col_pos = lax.axis_index("col")
    n_row = lax.axis_size("row")
    n_col = lax.axis_size("col")
    occ_a = amplitudes.shape[0]
    occ_h = amplitudes.shape[2]
    width_a = integrals.shape[0]
    pairs = occ_a * occ_h * n_row
    labels = jnp.repeat(irreps, VBLK)
    lab_a = lax.dynamic_slice_in_dim(labels, vir_pos * width_a, width_a)
    lab_c = labels[:CW]
    amp_rows = amplitudes.reshape(pairs, CW, NV)
    full_d = lax.all_gather(integrals, "col", axis=3, tiled=True)
    piece = lax.all_gather(full_d, "row", axis=1, tiled=True)
    lab_b = lax.slice_in_dim(labels, 0, piece.shape[1], axis=0)
    ladder = contract(amp_rows, masked_block(piece, lab_a, lab_b, lab_c, labels))
    slab_part = lax.dynamic_slice_in_dim(amplitudes, vir_pos * width_a, width_a, 6)
    every_k = lax.all_gather(slab_part, "col", axis=3, tiled=True).reshape(occ_a, NO, CW, width_a)
    hole_mat = hole_integrals.reshape(NO, occ_h * n_row, CW, SA)
    crossed = -lax.dot_general(
        every_k, hole_mat, (((1, 2), (0, 2)), ((), ())), preferred_element_type=jnp.float32
    )
    crossed = jnp.transpose(crossed, (0, 2, 1, 3)).reshape(pairs, width_a, SA)
    mixed = ladder + crossed
    groups = occ_a // n_col
    outgoing = mixed.reshape(groups, n_col, occ_h, n_row, width_a, SA)
    outgoing = jnp.transpose(outgoing, (3, 1, 0, 2, 4, 5)).reshape(
        n_row * n_col, groups, occ_h, width_a, SA
    )
    incoming = lax.all_to_all(
        lax.all_to_all(outgoing, ("row", "col"), split_axis=0, concat_axis=0, tiled=True),
        "vir",
        split_axis=4,
        concat_axis=3,
        tiled=True,
    )
    incoming = incoming.reshape(n_row, n_col, groups, occ_h, SA, width_a)
    mirrored = jnp.transpose(incoming, (3, 1, 2, 0, 5, 4)).reshape(pairs, width_a, SA)
    energy_i = lax.dynamic_slice_in_dim(occ_energy.reshape(occ_a, n_row), row_pos, 1, 1).reshape(
        occ_a
    )
    energy_j = lax.dynamic_slice_in_dim(
        occ_energy.reshape(occ_h, n_col, n_row), col_pos, 1, 1
    ).reshape(occ_h * n_row)
    energy_a = lax.dynamic_slice_in_dim(vir_energy, vir_pos * width_a, width_a)
    pair_sum = (energy_i[:, None] + energy_j[None, :]).reshape(pairs)
    denom = pair_sum[:, None, None] - energy_a[None, :, None] - vir_energy[None, None, :]
    result = ((mixed + mirrored) / denom).astype(jnp.bfloat16)
    return result.reshape(occ_a, 1, occ_h, 1, n_row, width_a, SA)


def solution(mesh):
    in_specs = (
        P(None, "row", None, "col", None, None, None),
        P("vir", "row", None, "col"),
        P(None, None, "col", None, None, None),
        P(),
        P(),
        P(),
    )
    out_specs = P(None, "row", None, "col", None, "vir", None)
    return jax.shard_map(local, mesh=mesh, in_specs=in_specs, out_specs=out_specs, check_vma=False)
```

profile of v0, /device:TPU:0, one launch (start us, length us, event | category | flops | bytes accessed | tf_op | source)
XLA Modules:
  0.0 1113.8 jit_solution(1989637203341858840)
XLA Ops:
  6.5 6.6 copy.35
  13.2 140.2 %all-gather.3.cloned.1.call-done = bf16[16,32,3,1792]{1,0,2,3:T(8,128)(2,1)} async-done(((bf16[16,32,3,448]{1,0,2,3:T(8,128)(2,1)}), bf16[16,32,3,1792]{1,0,2,3:T(8,128)(2,1)}) %all-gather.3.cloned.1.call-update) | async-done | bytes 5505040 | tf_op jit(solution)/shard_map/all_gather | solution.py:40
  153.4 28.9 %copy.36 = bf16[16,32,3,1792]{3,0,2,1:T(8,128)(2,1)} copy(bf16[16,32,3,1792]{1,0,2,3:T(8,128)(2,1)} %all-gather.3.cloned.1.call-done) | data formatting | bytes 11010048 | tf_op jit(solution)/shard_map/all_gather | solution.py:40
  182.8 21.4 %copy.37 = bf16[64,1,16,1,2,3,1792]{6,4,2,0,5,3,1:T(2,128)(2,1)} copy(bf16[64,1,16,1,2,3,1792]{6,4,5,3,2,1,0:T(2,128)(2,1)} %param.6) | data formatting | bytes 44040192 | tf_op args[0]
  204.2 3.3 constant_dynamic-slice_fusion
  207.5 39.4 %all_gather.11 = bf16[64,1,16,4,2,3,16]{6,4,5,3,2,1,0:T(2,128)(2,1)} all-gather(bf16[64,1,16,1,2,3,16]{6,4,5,3,2,1,0:T(2,128)(2,1)S(1)} %constant_dynamic-slice_fusion), channel_id=1, replica_groups=mesh['row'=2,'col'=4,'vir'=4] {'col'}, dimensions={3}, use_global_device_ids=true | all-gather | bytes 983040 | tf_op jit(solution)/shard_map/all_gather | solution.py:45
  246.9 14.8 %copy.39 = bf16[64,1,16,4,2,3,16]{0,6,5,4,3,2,1:T(8,128)(2,1)S(1)} copy(bf16[64,1,16,4,2,3,16]{6,4,5,3,2,1,0:T(2,128)(2,1)} %all_gather.11) | data formatting | bytes 1572864 | tf_op jit(solution)/shard_map/all_gather | solution.py:45
  261.7 2.0 copy.51
  263.8 9.3 bitcast_negate_fusion
  273.1 12.7 %copy.41 = f32[2048,16,64]{0,2,1:T(8,128)} copy(f32[2048,16,64]{2,1,0:T(8,128)} %bitcast.42) | data formatting | bytes 16777216 | tf_op jit(solution)/shard_map/reshape | solution.py:50
  285.8 44.1 %reshape.158 = bf16[2048,3,1792,1]{2,0,1,3:T(8,128)(2,1)} reshape(bf16[64,1,16,1,2,3,1792]{6,4,2,0,5,3,1:T(2,128)(2,1)} %copy.37) | data formatting | bytes 44040192 | tf_op jit(solution)/shard_map/reshape | solution.py:39
  330.1 11.2 %compare_select_fusion = bf16[16,64,3,1792]{3,0,2,1:T(8,128)(2,1)} fusion(bf16[16,64,3,1792]{3,0,2,1:T(8,128)(2,1)} %all-gather.5.cloned.1.call-done, s32[3,1792]{1,0:T(4,128)S(1)} %broadcast_xor_fusion.1, s32[16,64]{0,1:T(8,128)S(1)} %broadcast_xor_fusion), kind=kLoop, calls=%fused_computation.1 | loop fusion | flops 11010048 | bytes 22045696 | tf_op jit(solution)/shard_map/jit(_where)/select_n | solution.py:17
  341.2 31.3 %bitcast_add_fusion = f32[2048,16,64]{0,2,1:T(8,128)} fusion(f32[2048,16,64]{0,2,1:T(8,128)} %copy.41, bf16[2048,3,1792,1]{2,0,1,3:T(8,128)(2,1)} %reshape.158, bf16[16,64,3,1792]{3,0,2,1:T(8,128)(2,1)} %compare_select_fusion), kind=kOutput, calls=%fused_computation.5 | convolution fusion | flops 22550675456 | bytes 49807360 | tf_op jit(solution)/shard_map/dot_general | solution.py:21
  372.5 14.5 %copy.42 = f32[2048,16,64]{2,1,0:T(8,128)} copy(f32[2048,16,64]{0,2,1:T(8,128)} %bitcast_add_fusion) | data formatting | bytes 16777216 | tf_op jit(solution)/shard_map/add | solution.py:51
  387.0 11.7 %copy.43 = f32[2,4,16,16,16,64]{5,4,3,2,1,0:T(8,128)} copy(f32[2,4,16,16,16,64]{5,4,0,3,1,2:T(8,128)} %bitcast.45) | data formatting | bytes 16777216 | tf_op jit(solution)/shard_map/transpose | solution.py:54
  398.7 15.6 %reshape.172 = f32[8,1,262144]{2,1,0:T(1,128)} reshape(f32[8,16,16,16,64]{4,3,2,1,0:T(8,128)} %bitcast.43) | data formatting | bytes 16777216
  414.3 100.1 %all_to_all.20 = f32[8,1,262144]{2,1,0:T(1,128)} all-to-all(f32[8,1,262144]{2,1,0:T(1,128)} %reshape.172), channel_id=1, replica_groups=mesh['row'=2,'col'=4,'vir'=4] {'row','col'}, dimensions={0} | all-to-all | bytes 16777216 | tf_op jit(solution)/shard_map/all_to_all | solution.py:58
  514.5 0.5 broadcast.68
  515.0 26.2 %reduce.6 = f32[8,262144]{1,0:T(8,128)} reduce(f32[8,1,262144]{2,1,0:T(1,128)} %all_to_all.20, f32[]{:T(128)} %broadcast.68), dimensions={1}, to_apply=%all_to_all.14.reduce_sub_computation | reduce | bytes 16777220 | tf_op jit(solution)/shard_map/all_to_all | solution.py:58
  541.2 15.7 %reshape.173 = f32[8,16,16,16,64]{4,3,2,1,0:T(8,128)} reshape(f32[8,262144]{1,0:T(8,128)} %reduce.6) | data formatting | bytes 16777216
  556.9 50.4 %copy.44 = f32[8,16,16,16,64]{3,2,1,0,4:T(8,128)} copy(f32[8,16,16,16,64]{4,3,2,1,0:T(8,128)} %reshape.173) | data formatting | bytes 16777216 | tf_op jit(solution)/shard_map/all_to_all | solution.py:58
  607.3 52.9 %reshape.174 = f32[4,1,524288]{2,1,0:T(1,128)} reshape(f32[64,8,16,16,16]{4,3,2,1,0:T(8,128)} %bitcast.33) | data formatting | bytes 16777216
  660.2 5.8 all-to-all-start.1
  666.9 182.3 %all-to-all-done.1 = f32[4,1,524288]{2,1,0:T(1,128)} async-done(((f32[4,1,524288]{2,1,0:T(1,128)}), f32[4,1,524288]{2,1,0:T(1,128)}, u32[]{:S(2)}, u32[]{:S(2)}) %all-to-all-start.1) | async-done | bytes 8388640 | tf_op jit(solution)/shard_map/all_to_all | solution.py:57
  849.3 28.3 %reduce.7 = f32[4,524288]{1,0:T(4,128)} reduce(f32[4,1,524288]{2,1,0:T(1,128)} %all-to-all-done.1, f32[]{:T(128)} %broadcast.68), dimensions={1}, to_apply=%all_to_all.15.reduce_sub_computation | reduce | bytes 16777220 | tf_op jit(solution)/shard_map/all_to_all | solution.py:57
  877.6 61.5 %reshape.175 = f32[64,8,16,16,16]{4,3,2,1,0:T(8,128)} reshape(f32[4,524288]{1,0:T(4,128)} %reduce.7) | data formatting | bytes 16777216
  939.1 73.0 %copy.60 = f32[8,16,16,16,4,16]{3,4,5,2,1,0:T(4,128)} copy(f32[8,16,16,16,4,16]{3,2,1,0,5,4:T(8,128)} %bitcast.14) | data formatting | bytes 16777216 | tf_op jit(solution)/shard_map/all_to_all | solution.py:57
  1012.1 50.1 %reshape.153 = f32[2,4,16,16,64,16]{4,5,3,2,1,0:T(8,128)} reshape(f32[8,16,16,4,16,16]{4,3,5,2,1,0:T(4,128)} %bitcast.38) | data formatting | bytes 16777216 | tf_op jit(solution)/shard_map/reshape | solution.py:64
  1062.3 12.0 %copy.46 = f32[16,4,16,2,16,64]{5,4,3,2,1,0:T(8,128)} copy(f32[16,4,16,2,16,64]{5,4,0,2,1,3:T(8,128)} %bitcast.41) | data formatting | bytes 16777216 | tf_op jit(solution)/shard_map/transpose | solution.py:65
  1074.2 12.8 %copy.47 = f32[2048,16,64]{0,2,1:T(8,128)} copy(f32[2048,16,64]{2,1,0:T(8,128)} %bitcast.44) | data formatting | bytes 16777216 | tf_op jit(solution)/shard_map/reshape | solution.py:65
  1087.0 8.9 divide_convert_fusion
  1095.9 10.9 copy.48
  (37 shorter events, 1.5 us)
Async XLA Ops:
  6.5 257.2 %copy-start = (bf16[128,16,1,2,3,64]{0,5,4,3,2,1:T(8,128)(2,1)S(1)}, bf16[128,16,1,2,3,64]{0,5,4,3,2,1:T(8,128)(2,1)}, u32[]{:S(2)}) copy-start(bf16[128,16,1,2,3,64]{0,5,4,3,2,1:T(8,128)(2,1)} %param.8) | copy-start | bytes 4718596
  6.5 146.9 %all-gather.3.cloned.1.call-start = ((), (), s32[]{:S(2)}) async-start(), calls=%async_computation.2 | async-start | bytes 27525120 | tf_op jit(solution)/shard_map/all_gather | solution.py:40
  13.2 169.2 %copy-start.5 = (s32[112]{0:T(128)S(1)}, s32[112]{0:T(128)}, u32[]{:S(2)}) copy-start(s32[112]{0:T(128)} %param.9) | copy-start | bytes 1348
  13.2 316.9 %all-gather.5.cloned.1.call-start = ((), (), s32[]{:S(2)}) async-start(), calls=%async_computation.3 | async-start | bytes 16515072 | tf_op jit(solution)/shard_map/all_gather | solution.py:41
  182.6 21.7 %copy-start.2 = (s32[1792]{0:T(1024)}, s32[1792]{0:T(1024)S(1)}, u32[]{:S(2)}) copy-start(s32[1792]{0:T(1024)S(1)} %reshape.146) | copy-start | bytes 21508
  285.8 44.2 %copy-start.3 = (s32[1792]{0:T(1024)S(1)}, s32[1792]{0:T(1024)}, u32[]{:S(2)}) copy-start(s32[1792]{0:T(1024)} %copy-done.2) | copy-start | bytes 21508
  285.8 44.2 %slice-start = ((s32[1792]{0:T(1024)}), s32[3]{0:T(128)S(1)}, s32[]{:S(2)}) async-start(s32[1792]{0:T(1024)} %copy-done.2), calls=%async_computation.4 | async-start | bytes 1024 | tf_op jit(solution)/shard_map/slice | solution.py:38
  660.2 5.8 copy-start.4
  660.2 6.6 copy-start.6
  660.2 189.1 %all-to-all-start.1 = ((f32[4,1,524288]{2,1,0:T(1,128)}), f32[4,1,524288]{2,1,0:T(1,128)}, u32[]{:S(2)}, u32[]{:S(2)}) async-start(f32[4,1,524288]{2,1,0:T(1,128)} %reshape.174), calls=%async_computation.1 | async-start | bytes 16777216 | tf_op jit(solution)/shard_map/all_to_all | solution.py:57
  1087.0 19.8 %copy-start.1 = (bf16[128,16,1,2,3,64]{0,5,4,3,2,1:T(8,128)(2,1)S(1)}, bf16[128,16,1,2,3,64]{0,5,4,3,2,1:T(8,128)(2,1)}, u32[]{:S(2)}) copy-start(bf16[128,16,1,2,3,64]{0,5,4,3,2,1:T(8,128)(2,1)} %param.8) | copy-start | bytes 4718596
Sparse Core Ops, SparseCore 0:
  13.3 140.1 all-gather.2
  182.5 135.2 all-gather.4
where the time goes:
time: 1120 us; the launch traced here: 1110 us
  local copies, waits for them, and re-layouts  517 us (46%)
  waiting for transfers between devices  323 us (29%)
  blocking collectives  140 us (12%)
  other arithmetic  74.8 us (7%)
  matrix products  40.6 us (4%)
  between operations  13.7 us (1%)
    all_to_all x1, waiting for transfers between devices, local(): lax.all_to_all(lax.all_to_all(outgoing, ('row', 'col'), split_axis=0, con...  182 us
    unnamed x20, local copies, waits for them, and re-layouts  174 us
    all_gather x1, waiting for transfers between devices, local(): full_d = lax.all_gather(integrals, 'col', axis=3, tiled=True)  140 us
    all_to_all x1, blocking collectives, local(): lax.all_to_all(outgoing, ('row', 'col'), split_axis=0, concat_axis=0, til...  100 us
    all_to_all x1, local copies, waits for them, and re-layouts, local(): lax.all_to_all(lax.all_to_all(outgoing, ('row', 'col'), split_axis=0, con...  73 us
    all_to_all x2, local copies, waits for them, and re-layouts, local(): lax.all_to_all(outgoing, ('row', 'col'), split_axis=0, concat_axis=0, til...  51 us
    reshape x1, local copies, waits for them, and re-layouts, local(): incoming = incoming.reshape(n_row, n_col, groups, occ_h, SA, width_a)  50.1 us
    reshape x1, local copies, waits for them, and re-layouts, local(): amp_rows = amplitudes.reshape(pairs, CW, NV)  44.1 us
  transfers between devices with their start and end apart: 3, of which 2 were waited for; matrix products, arithmetic and copies ran while one was open for 10% of the time, Pallas kernels for 0%

commit v1 on v0

--- a/solution.py
+++ b/solution.py
@@ -1,6 +1,11 @@
+import functools
+
 import jax
 import jax.numpy as jnp
+import numpy as np
 from jax import lax
+from jax.experimental import pallas as pl
+from jax.experimental.pallas import tpu as pltpu
 from jax.sharding import PartitionSpec as P
 
 NO = 128
@@ -9,6 +14,544 @@
 CW = 3
 VBLK = 16
 
+LANES = 128
+WIDE = VBLK * VBLK
+ROOM = 10
+AXES = ("row", "col", "vir")
+BF = jnp.bfloat16
+F32 = jnp.float32
+GRAIN = 64.0
+TOP = 32000.0
+PARAMS = pltpu.CompilerParams(vmem_limit_bytes=56 * 1024 * 1024)
+ANY = pl.BlockSpec(memory_space=pl.ANY)
+PLACE = [b // 8 * 8 + b % 2 * 4 + b % 8 // 2 for b in range(VBLK)]
+NAMED = [PLACE.index(p) for p in range(VBLK)]
+
+
+def nt(left, right):
+    return lax.dot_general(left, right, (((1,), (1,)), ((), ())), preferred_element_type=F32)
+
+
+def cost(flops, moved):
+    return pl.CostEstimate(flops=int(flops), bytes_accessed=int(moved), transcendentals=0)
+
+
+def pack_kernel(spot_ref, irr_ref, turn_ref, v_ref, out_ref):
+    depth = v_ref.shape[3]
+    count = depth // VBLK
+    lane = lax.broadcasted_iota(jnp.int32, (1, depth), 1)
+    row = lax.broadcasted_iota(jnp.int32, (ROOM * VBLK, depth), 0)
+    for half in range(2):
+        label = irr_ref[spot_ref[2]] ^ irr_ref[2 * spot_ref[0] + half] ^ irr_ref[0]
+        held = -spot_ref[3]
+        target = jnp.full((1, depth), -1, jnp.int32)
+        for block in range(count):
+            match = irr_ref[spot_ref[1] * count + block] == label
+            start = jnp.where(match & (held >= 0), held * VBLK, -NV)
+            target = jnp.where(lane // VBLK == block, start + lane % VBLK, target)
+            held = held + match.astype(jnp.int32)
+        pick = (row == target).astype(F32).astype(BF)
+        for c in range(CW):
+            part = v_ref[:, c, half * VBLK : (half + 1) * VBLK, :].reshape(WIDE, depth)
+            packed = nt(pick, part).astype(BF)
+            out_ref[half, c] = jnp.dot(packed, turn_ref[...], preferred_element_type=F32).astype(BF)
+
+
+def pack(spot, irreps, turn, v):
+    return pl.pallas_call(
+        pack_kernel,
+        grid_spec=pltpu.PrefetchScalarGridSpec(
+            num_scalar_prefetch=2,
+            grid=(1,),
+            in_specs=[
+                pl.BlockSpec(turn.shape, lambda i, *_: (0, 0)),
+                pl.BlockSpec(v.shape, lambda i, *_: (0, 0, 0, 0)),
+            ],
+            out_specs=pl.BlockSpec((2, CW, ROOM * VBLK, WIDE), lambda i, *_: (0, 0, 0, 0)),
+        ),
+        out_shape=jax.ShapeDtypeStruct((2, CW, ROOM * VBLK, WIDE), BF),
+        compiler_params=PARAMS,
+        cost_estimate=cost(4e8, 2e6),
+    )(spot, irreps, turn, v)
+
+
+def unpack_kernel(n_col, spot_ref, irr_ref, near_ref, far_ref, out_ref, found_ref):
+    step = pl.program_id(0)
+    other = spot_ref[2] ^ jnp.where(step == 0, 3, step - 1)
+    label = irr_ref[spot_ref[2]] ^ irr_ref[other] ^ irr_ref[0]
+    away = ((other // 2) != spot_ref[0]).astype(jnp.int32)
+    base = jnp.where(step == 0, 8, away * 4 + other % 2)
+    pace = jnp.where(step == 0, 1, 2)
+    depth = NV // n_col
+    count = depth // VBLK
+    out_ref[...] = jnp.zeros(out_ref.shape, BF)
+    for dc in range(n_col):
+        shard = spot_ref[1] ^ dc
+        piece_ref = far_ref if dc % 2 else near_ref
+        which = base + (dc // 2) * pace
+
+        def note(block, held):
+            found_ref[jnp.clip(held + 1, 0, ROOM + 1)] = block
+            return held + (irr_ref[shard * count + block] == label).astype(jnp.int32)
+
+        held = lax.fori_loop(0, count, note, -spot_ref[3], unroll=count)
+
+        def move(place, _):
+            row = shard * depth + found_ref[place + 1] * VBLK
+            for c in range(CW):
+                out_ref[pl.ds(pl.multiple_of(c * NV + row, VBLK), VBLK), :] = piece_ref[
+                    which, c, pl.ds(pl.multiple_of(place * VBLK, VBLK), VBLK), :
+                ]
+            return 0
+
+        lax.fori_loop(0, jnp.clip(held, 0, ROOM), move, 0)
+
+
+def unpack(spot, irreps, near, far, n_col):
+    whole = pl.BlockSpec(near.shape, lambda t, *_: (0, 0, 0, 0))
+    return pl.pallas_call(
+        functools.partial(unpack_kernel, n_col),
+        grid_spec=pltpu.PrefetchScalarGridSpec(
+            num_scalar_prefetch=2,
+            grid=(5,),
+            in_specs=[whole, whole],
+            out_specs=pl.BlockSpec((CW * NV, WIDE), lambda t, *_: (0, t)),
+            scratch_shapes=[pltpu.SMEM((ROOM + 2,), jnp.int32)],
+        ),
+        out_shape=jax.ShapeDtypeStruct((CW * NV, 5 * WIDE), BF),
+        compiler_params=PARAMS,
+        cost_estimate=cost(1e6, 18e6),
+    )(spot, irreps, near, far)
+
+
+def chunk_kernel(spot_ref, t_ref, out_ref, slab_ref):
+    groups, occ_h = t_ref.shape[0], t_ref.shape[2]
+    rows = 2 * occ_h
+    first = []
+    for c in range(CW):
+        part = t_ref[:, 0, :, c, :, :].reshape(groups * rows, NV)
+        out_ref[0, :, c * NV : (c + 1) * NV] = part
+        first.append(part[:, :LANES])
+    row = lax.broadcasted_iota(jnp.int32, (2 * VBLK, LANES), 0)
+    lane = lax.broadcasted_iota(jnp.int32, (2 * VBLK, LANES), 1)
+    block = jnp.where(row < VBLK, spot_ref[2], spot_ref[2] ^ 3)
+    pick = (lane == block * VBLK + row % VBLK).astype(F32).astype(BF)
+    empty = jnp.zeros((rows, LANES), BF)
+    for q in range(groups):
+        some = jnp.concatenate([x[q * rows : (q + 1) * rows] for x in first] + [empty], axis=0)
+        found = nt(pick, some).astype(BF)
+        for far in range(2):
+            slab_ref[far, 0, q * VBLK : (q + 1) * VBLK, :] = found[far * VBLK : (far + 1) * VBLK]
+
+
+def chunk_amplitudes(spot, t, dcs):
+    q4, n_col, occ_h, _, n_row, _ = t.shape
+    some = 4
+    rows = occ_h * n_row
+
+    def group(i, spot):
+        return spot[1] ^ jnp.where(i == 0, dcs[0], dcs[-1])
+
+    return pl.pallas_call(
+        chunk_kernel,
+        grid_spec=pltpu.PrefetchScalarGridSpec(
+            num_scalar_prefetch=1,
+            grid=(len(dcs), q4 // some),
+            in_specs=[
+                pl.BlockSpec(
+                    (some, 1, occ_h, CW, n_row, NV), lambda i, q, spot: (q, group(i, spot), 0, 0, 0, 0)
+                )
+            ],
+            out_specs=[
+                pl.BlockSpec((1, some * rows, CW * NV), lambda i, q, _: (i, q, 0)),
+                pl.BlockSpec((2, 1, some * VBLK, LANES), lambda i, q, _: (0, i, q, 0)),
+            ],
+        ),
+        out_shape=[
+            jax.ShapeDtypeStruct((len(dcs), q4 * rows, CW * NV), BF),
+            jax.ShapeDtypeStruct((2, len(dcs), q4 * VBLK, LANES), BF),
+        ],
+        compiler_params=PARAMS,
+        cost_estimate=cost(1e8, 23e6),
+    )(spot, t)
+
+
+def trade_lanes(x, bits):
+    piece = lax.broadcasted_iota(jnp.int32, x[0].shape, 1) // VBLK
+    for k in range(bits):
+        bit = 1 << k
+        upper = (piece & bit) != 0
+        y = []
+        for i in range(1 << bits):
+            if i & bit:
+                moved = pltpu.roll(x[i ^ bit], LANES - bit * VBLK, 1)
+                y.append(jnp.where(upper, x[i], moved))
+            else:
+                moved = pltpu.roll(x[i ^ bit], bit * VBLK, 1)
+                y.append(jnp.where(upper, moved, x[i]))
+        x = y
+    return x
+
+
+def mixed_kernel(n_col, spot_ref, t_ref, v_ref, w_ref, order_ref, *refs):
+    parts, refs = refs[:n_col], refs[n_col:]
+    u_ref, near0_ref, near1_ref, one_ref, two_ref, acc, zs, ints, slabs = refs
+    step = pl.program_id(0)
+    rows = 2 * WIDE
+
+    def product():
+        return jnp.dot(t_ref[0], v_ref[...], preferred_element_type=F32)
+
+    def keep(ladder):
+        for half in range(2):
+            acc[half] = ladder[:, half * LANES : (half + 1) * LANES]
+
+    def rest():
+        holes = jnp.concatenate([w_ref[:, c].reshape(rows, NO) for c in range(CW)], axis=1)
+        slab = slabs[(step == 1).astype(jnp.int32)]
+        cross = jnp.dot(holes, slab, preferred_element_type=F32)
+        for half in range(2):
+            zs[half] = cross[:, half * LANES : (half + 1) * LANES]
+        for lt in range(2):
+            for s in range(2):
+                for half in range(2):
+                    for hh in range(2):
+                        first = [
+                            s * WIDE + NAMED[half * 8 + i] * VBLK + hh * 8 for i in range(8)
+                        ]
+                        x = trade_lanes([zs[lt, at : at + 8, :] for at in first], 3)
+                        for j in range(8):
+                            q4 = lt * 8 + j
+                            have = acc[half, pl.ds(q4 * 32 + hh * 16 + s, 8, stride=2), :]
+                            u_ref[
+                                s, q4 * 16 + hh * 8 : q4 * 16 + hh * 8 + 8,
+                                half * LANES : (half + 1) * LANES,
+                            ] = have - x[j]
+        for dr in range(2):
+            value = u_ref[spot_ref[0] ^ dr]
+            most = jnp.maximum(jnp.max(jnp.abs(value), axis=0, keepdims=True), 1e-30)
+            grade = jnp.ceil(jnp.log2(most) * GRAIN)
+            scale = TOP * jnp.exp2(-grade / GRAIN)
+            whole = jnp.floor(value * scale + 0.5).astype(jnp.int32).astype(jnp.int16)
+            grades = jnp.broadcast_to(grade, (16, WIDE)).astype(jnp.int32).astype(jnp.int16)
+            ints[dr, :WIDE, :] = whole
+            ints[dr, WIDE:, :] = grades
+
+    @pl.when(step == 0)
+    def _():
+        order = jnp.concatenate([order_ref[spot_ref[1] ^ dc] for dc in range(n_col)], axis=1)
+        for far in range(2):
+            pieces = jnp.concatenate([part[0, far, 0] for part in parts], axis=1)
+            slabs[far] = nt(order, pieces).astype(BF)
+        keep(product())
+
+    @pl.when((step > 0) & (step < 5))
+    def _():
+        ladder = product()
+        rest()
+        keep(ladder)
+
+    @pl.when(step == 5)
+    def _():
+        rest()
+
+    def send(outs):
+        for dr in range(2):
+            outs[dr][...] = ints[dr]
+
+    for n, outs in (
+        (1, (near0_ref.at[1], near1_ref.at[1])),
+        (2, (near0_ref.at[0], near1_ref.at[0])),
+        (3, (one_ref.at[0], one_ref.at[1])),
+        (4, (two_ref.at[0], two_ref.at[1])),
+    ):
+        pl.when(step == n)(functools.partial(send, outs))
+
+
+def mixed_group(dc, spot, t, at, v, w, order, near, far, n_col):
+    ints = jax.ShapeDtypeStruct((2, WIDE + 16, WIDE), jnp.int16)
+    ints_spec = pl.BlockSpec(ints.shape, lambda n, spot: (0, 0, 0))
+
+    def slab_spec(other):
+        group = dc ^ other
+        which = (2 if group % 2 == 0 else 0) + other // 2
+        return pl.BlockSpec(
+            (1, 2, 1, WIDE, LANES), lambda n, spot: (which, 0, int(group < 2), 0, 0)
+        )
+
+    return pl.pallas_call(
+        functools.partial(mixed_kernel, n_col),
+        grid_spec=pltpu.PrefetchScalarGridSpec(
+            num_scalar_prefetch=1,
+            grid=(6,),
+            in_specs=[
+                pl.BlockSpec((1,) + t.shape[1:], lambda n, spot: (at, 0, 0)),
+                pl.BlockSpec((CW * NV, WIDE), lambda n, spot: (0, jnp.minimum(n, 4))),
+                pl.BlockSpec(
+                    (2, CW, VBLK, w.shape[3], NO),
+                    lambda n, spot: (0, 0, spot[2] ^ jnp.maximum(n - 2, 0), 0, 0),
+                ),
+                pl.BlockSpec(order.shape, lambda n, spot: (0, 0, 0)),
+            ]
+            + [slab_spec(other) for other in range(n_col)],
+            out_specs=[
+                pl.BlockSpec((2, WIDE, WIDE), lambda n, spot: (0, 0, jnp.clip(n - 2, 0, 3)))
+            ]
+            + [ints_spec] * 4,
+            scratch_shapes=[
+                pltpu.VMEM((2, 2 * WIDE, LANES), F32),
+                pltpu.VMEM((2, 2 * WIDE, LANES), F32),
+                pltpu.VMEM((2, WIDE + 16, WIDE), jnp.int16),
+                pltpu.VMEM((2, CW * NO, WIDE), BF),
+            ],
+        ),
+        out_shape=[jax.ShapeDtypeStruct((2, WIDE, 4 * WIDE), F32)] + [ints] * 4,
+        compiler_params=PARAMS,
+        cost_estimate=cost(7.2e9, 24e6),
+    )(spot, t, v, w, order, *([near, far] * 2))
+
+
+def trade_rows(x):
+    row = lax.broadcasted_iota(jnp.int32, x[0].shape, 0)
+    for k in range(3):
+        bit = 1 << k
+        upper = (row & bit) != 0
+        y = []
+        for i in range(8):
+            if i & bit:
+                y.append(jnp.where(upper, x[i], pltpu.roll(x[i ^ bit], 8 - bit, 0)))
+            else:
+                y.append(jnp.where(upper, pltpu.roll(x[i ^ bit], bit, 0), x[i]))
+        x = y
+    return x
+
+
+def final_kernel(spot_ref, pair_ref, slab_ref, turn_ref, swap_ref, u_ref, *refs):
+    got, (out_ref, ints, incs, os) = refs[:5], refs[-4:]
+    step = pl.program_id(0)
+    for dr in range(2):
+
+        @pl.when(step == dr)
+        def _(dr=dr):
+            if dr == 0:
+                near, one, two = got[0], got[1].at[0], got[2].at[0]
+            else:
+                near, one, two = got[3], got[4].at[0], got[4].at[1]
+            ints[0], ints[1], ints[2], ints[3] = near[0], one[...], two[...], near[1]
+
+    own = u_ref[0]
+    high = own.astype(BF)
+    low = (own - high.astype(F32)).astype(BF)
+    both = jnp.concatenate([high, low], axis=1)
+    both = jnp.dot(turn_ref[...], both, preferred_element_type=F32).astype(BF)
+    both = jnp.concatenate([both[:, i * WIDE : (i + 1) * WIDE] for i in range(8)], axis=0)
+    both = jnp.dot(both, swap_ref[...], preferred_element_type=F32)
+    pair = pair_ref[0, 0]
+    for t in range(4):
+        mine = both[t * WIDE : (t + 1) * WIDE] + both[(t + 4) * WIDE : (t + 5) * WIDE]
+        grade = ints[t, WIDE : WIDE + 16, :].astype(jnp.int32).astype(F32)[:1]
+        scale = jnp.exp2(grade / GRAIN) / TOP
+        mirror = ints[t, :WIDE, :].astype(jnp.int32).astype(F32) * scale
+        incs[t] = (mine + mirror) / (pair - slab_ref[:, t * WIDE : (t + 1) * WIDE])
+    for h in range(16):
+        for q_half in range(2):
+            rows = slice(h * 16 + q_half * 8, h * 16 + q_half * 8 + 8)
+            x = []
+            for half in range(2):
+                lanes = slice(half * LANES, (half + 1) * LANES)
+                x += trade_lanes([incs[spot_ref[2] ^ b, rows, lanes] for b in range(4)], 2)
+            for p, pieces in enumerate(trade_rows(x)):
+                first = ((q_half * 8 + p) * 16 + h) * VBLK
+                os[pl.ds(first, 8, stride=2), :] = pieces
+                os[pl.ds(first + 1, 8, stride=2), :] = pltpu.roll(pieces, SA, 1)
+    out_ref[...] = os[...][:, :SA].astype(BF).reshape(out_ref.shape)
+
+
+def final_group(dc, spot, pair, slab, turn, swap, u, got, out):
+    near_spec = pl.BlockSpec((2, WIDE + 16, WIDE), lambda i, spot: (0, 0, 0))
+    far_spec = pl.BlockSpec((1, WIDE + 16, WIDE), lambda i, spot: (0, 0, 0))
+    more = [] if out is None else [out]
+    return pl.pallas_call(
+        final_kernel,
+        grid_spec=pltpu.PrefetchScalarGridSpec(
+            num_scalar_prefetch=1,
+            grid=(2,),
+            in_specs=[
+                pl.BlockSpec((1, 1, WIDE, 1), lambda i, spot: (spot[1] ^ dc, i ^ spot[0], 0, 0)),
+                pl.BlockSpec(slab.shape, lambda i, spot: (0, 0)),
+                pl.BlockSpec(turn.shape, lambda i, spot: (0, 0)),
+                pl.BlockSpec(swap.shape, lambda i, spot: (0, 0)),
+                pl.BlockSpec((1, WIDE, 4 * WIDE), lambda i, spot: (i ^ spot[0], 0, 0)),
+            ]
+            + [near_spec, far_spec, far_spec, near_spec, near_spec]
+            + [ANY] * len(more),
+            out_specs=pl.BlockSpec(
+                (16, 1, 16, 1, VBLK, SA), lambda i, spot: (0, spot[1] ^ dc, 0, i ^ spot[0], 0, 0)
+            ),
+            scratch_shapes=[
+                pltpu.VMEM((4, WIDE + 16, WIDE), jnp.int16),
+                pltpu.VMEM((4, WIDE, WIDE), F32),
+                pltpu.VMEM((WIDE * VBLK, LANES), F32),
+            ],
+        ),
+        out_shape=jax.ShapeDtypeStruct((16, 4, 16, 2, VBLK, SA), BF),
+        input_output_aliases={11: 0} if more else {},
+        compiler_params=PARAMS,
+        cost_estimate=cost(2e9, 10e6),
+    )(spot, pair, slab, turn, swap, u, *got, *more)
+
+
+def partners(sizes, row, col, vir):
+    n_row, n_col, n_vir = sizes
+    found = []
+    for r in range(n_row):
+        for c in range(n_col):
+            for z in range(n_vir):
+                mine = (r * n_col + c) * n_vir + z
+                other = ((r ^ row) * n_col + (c ^ col)) * n_vir + (z ^ vir)
+                found.append((mine, other))
+    return found
+
+
+def packed_local(amplitudes, integrals, hole_integrals, irreps, occ_energy, vir_energy):
+    vir_pos = lax.axis_index("vir")
+    row_pos = lax.axis_index("row")
+    col_pos = lax.axis_index("col")
+    sizes = tuple(lax.axis_size(axis) for axis in AXES)
+    n_row, n_col, n_vir = sizes
+    occ_a, occ_h = amplitudes.shape[0], amplitudes.shape[2]
+    groups = occ_a // n_col
+
+    def swap_with(value, row, col, vir):
+        if not (row or col or vir):
+            return value
+        return lax.ppermute(value, AXES, partners(sizes, row, col, vir))
+
+    def place(first):
+        return jnp.stack([row_pos, col_pos, vir_pos, first]).astype(jnp.int32)
+
+    spot = place(0)
+    high, low = np.arange(WIDE) // VBLK, np.arange(WIDE) % VBLK
+    place_of, named = np.array(PLACE), np.array(NAMED)
+    eye = np.eye(WIDE, dtype=np.float32)
+    flip = jnp.asarray(eye[low * VBLK + high], BF)
+    by_b = jnp.asarray(eye[place_of[low] * VBLK + high], BF)
+    swap = jnp.asarray(eye[place_of[low] * VBLK + named[high]], BF)
+    shard = jnp.transpose(integrals, (0, 2, 1, 3))
+
+    def later(spot, *values):
+        spot, *values = lax.optimization_barrier((spot, *values))
+        return spot, *values
+
+    def gather(mine, beside=lambda values: values, after=lambda values: values):
+        over = lax.dynamic_index_in_dim(mine, (vir_pos ^ 3) % 2, 0, True)
+        across, beyond = swap_with(mine, 0, 2, 0), swap_with(mine, 1, 0, 0)
+        overs = [swap_with(over, 0, 0, 3), swap_with(over, 1, 0, 3)]
+        across, *overs = beside([across, *overs])
+        over = jnp.where(vir_pos // 2 == row_pos, *overs)
+        near = [across, beyond, swap_with(across, 1, 0, 0), over, swap_with(over, 0, 2, 0)]
+        near = jnp.concatenate([mine] + after(near), axis=0)
+        return near, swap_with(near, 0, 1, 0)
+
+    every = irreps.reshape(1, n_col, -1) == jnp.arange(8, dtype=irreps.dtype)[:, None, None]
+    fullest = jnp.max(jnp.sum(every.astype(jnp.int32), axis=-1))
+
+    energy_i = lax.dynamic_index_in_dim(occ_energy.reshape(groups, n_col, n_row), row_pos, 2, False)
+    energy_j = lax.dynamic_index_in_dim(occ_energy.reshape(occ_h, n_col, n_row), col_pos, 1, False)
+    pair = energy_i.T[:, None, None, :] + energy_j.T[None, :, :, None]
+    pair = pair.reshape(n_col, n_row, occ_h * groups, 1)
+    energies = vir_energy.reshape(n_vir, VBLK)
+    energy_a = lax.dynamic_index_in_dim(energies, vir_pos, 0, False)[named]
+    energy_b = jnp.take(energies, vir_pos ^ jnp.arange(n_vir), axis=0)
+    slab_sum = (energy_a[None, :, None] + energy_b[:, None, :]).reshape(1, n_vir * WIDE)
+
+    mine = pack(spot, irreps, by_b, shard)
+    spot, mine = later(spot, mine)
+
+    amps = jnp.transpose(amplitudes.reshape(groups, n_col, occ_h, n_row, CW, NV), (0, 1, 2, 4, 3, 5))
+    first, slab = chunk_amplitudes(spot, amps, (3, 1))
+    spot, first, slab = later(spot, first, slab)
+    state = {"spot": spot, "slabs": [slab, swap_with(slab, 0, 2, 0)]}
+
+    def hold(values):
+        state["spot"], *values = later(state["spot"], *values)
+        return values
+
+    def hold_second(values):
+        state["second"], slab = chunk_amplitudes(state["spot"], amps, (2, 0))
+        state["spot"], state["second"], slab = later(state["spot"], state["second"], slab)
+        *values, state["slabs"][1] = hold([*values, state["slabs"][1]])
+        state["slabs"] += [slab, swap_with(slab, 0, 2, 0)]
+        return values
+
+    near, far = gather(mine, hold, hold_second)
+    spot, slabs = state["spot"], state["slabs"]
+    holes = jnp.transpose(hole_integrals.reshape(NO, occ_h, n_row, CW, SA), (2, 3, 4, 1, 0))
+    spot, near, holes, pair, slab_sum, fullest = later(spot, near, holes, pair, slab_sum, fullest)
+    rows_of = [(first, 0), (first, 1), (state["second"], 0), (state["second"], 1)]
+    spot, far, slabs[3] = later(spot, far, slabs[3])
+    slabs = jnp.stack(slabs)
+    slabs_far = swap_with(slabs, 0, 1, 0)
+    dense = unpack(spot, irreps, near, far, n_col)
+    dense, slabs_far = lax.optimization_barrier((dense, slabs_far))
+
+    k = np.arange(NO)
+    order = np.zeros((n_col, CW, NO, LANES), np.float32)
+    per_shard = NO // n_col
+    for c in range(CW):
+        lane = c * per_shard + (k // (n_row * n_col)) * n_row + k % n_row
+        order[(k // n_row) % n_col, c, k, lane] = 1
+    order = jnp.asarray(order.reshape(n_col, CW * NO, LANES), BF)
+
+    def another(first):
+        here = place(first)
+        near, far = gather(pack(here, irreps, by_b, shard))
+        return unpack(here, irreps, near, far, n_col)
+
+    dense = lax.while_loop(
+        lambda state: state[0] < fullest,
+        lambda state: (state[0] + ROOM, state[1] + another(state[0])),
+        (jnp.int32(ROOM), dense),
+    )[1]
+
+    def sum_group(chunk, spot, out):
+        dc, u, got = chunk
+        return final_group(dc, spot, pair, slab_sum, flip, swap, u, got, out)
+
+    def arrive(chunk, spot, *waited):
+        held = [chunk[2][name] for name in waited]
+        spot, held = lax.optimization_barrier((spot, held))
+        chunk[2].update(zip(waited, held))
+        far = chunk[2]["far"]
+        on = swap_with(jnp.stack([piece[1] for piece in far]), 1, 0, 0)
+        chunk[2] = [chunk[2]["near"][0], *far, chunk[2]["near"][1], on]
+        return spot
+
+    out = None
+    chunks = []
+    for turn, dc in enumerate((3, 1, 2, 0)):
+        if turn >= 2:
+            spot = arrive(chunks[turn - 2], spot, "near", "far")
+        if turn == 3:
+            out = sum_group(chunks[0], spot, out)
+            spot, out = lax.optimization_barrier((spot, out))
+        u, near0, near1, one, two = mixed_group(
+            dc, spot, *rows_of[turn], dense, holes, order, slabs, slabs_far, n_col
+        )
+        sent = {
+            "near": [swap_with(near0, 0, dc, 0), swap_with(near1, 1, dc, 0)],
+            "far": [swap_with(one, 0, dc, 1), swap_with(two, 0, dc, 2)],
+        }
+        spot, u = lax.optimization_barrier((spot, u))
+        chunks.append([dc, u, sent])
+    spot = arrive(chunks[2], spot, "near", "far")
+    out = sum_group(chunks[1], spot, out)
+    spot, out = lax.optimization_barrier((spot, out))
+    spot = arrive(chunks[3], spot, "far")
+    for turn in (2, 3):
+        out = sum_group(chunks[turn], spot, out)
+    return out.reshape(occ_a, 1, occ_h, 1, n_row, VBLK, SA)
+
 
 def masked_block(piece, lab_a, lab_b, lab_c, lab_d):
     left = jnp.bitwise_xor(lab_a[:, None], lab_b[None, :])
@@ -23,7 +566,7 @@
     )
 
 
-def local(amplitudes, integrals, hole_integrals, irreps, occ_energy, vir_energy):
+def plain_local(amplitudes, integrals, hole_integrals, irreps, occ_energy, vir_energy):
     vir_pos = lax.axis_index("vir")
     row_pos = lax.axis_index("row")
     col_pos = lax.axis_index("col")
@@ -86,4 +629,6 @@
         P(),
     )
     out_specs = P(None, "row", None, "col", None, "vir", None)
-    return jax.shard_map(local, mesh=mesh, in_specs=in_specs, out_specs=out_specs, check_vma=False)
+    sizes = tuple(mesh.shape[axis] for axis in AXES)
+    body = packed_local if sizes == (2, 4, 4) else plain_local
+    return jax.shard_map(body, mesh=mesh, in_specs=in_specs, out_specs=out_specs, check_vma=False)

time: 1120 us -> 207 us (0.18)
  local copies, waits for them, and re-layouts: 517 us -> 13 us
  waiting for transfers between devices: 323 us -> 4.3 us
  blocking collectives: 140 us -> 0 us
  Pallas kernels: 0 us -> 139 us
  other arithmetic: 74.8 us -> 4.06 us
  matrix products: 40.6 us -> 0 us
  starting transfers between devices: 5.82 us -> 44.7 us
  between operations: 13.7 us -> 0.64 us
    all_to_all x1 -> x0, waiting for transfers between devices: 182 us -> none  [local(): lax.all_to_all(lax.all_to_all(outgoing, ('row', 'col'), split_axis=0, con...]
    unnamed x20 -> x68, local copies, waits for them, and re-layouts: 174 us -> 9.21 us
    all_gather x2 -> x0, waiting for transfers between devices: 140 us -> none  [the longest x1 140 us: local(): full_d = lax.all_gather(integrals, 'col', axis=3, tiled=True)]
    pallas_call x0 -> x12, Pallas kernels: none -> 139 us  [the longest x4 71.8 us: mixed_group(): pl.pallas_call(functools.partial(mixed_kernel, n_col), grid_spec=pltpu.Pr...]
    all_to_all x3 -> x0, local copies, waits for them, and re-layouts: 124 us -> none  [the longest x1 73 us: local(): lax.all_to_all(lax.all_to_all(outgoing, ('row', 'col'), split_axis=0, con...]
    reshape x8 -> x2, local copies, waits for them, and re-layouts: 122 us -> 0.24 us  [the longest x1 0.16 us: packed_local(): occ_energy.reshape(groups, n_col, n_row)]
    all_to_all x1 -> x0, blocking collectives: 100 us -> none  [local(): lax.all_to_all(outgoing, ('row', 'col'), split_axis=0, concat_axis=0, til...]
    all_to_all x2 -> x0, other arithmetic: 54.5 us -> none  [the longest x1 28.3 us: local(): lax.all_to_all(lax.all_to_all(outgoing, ('row', 'col'), split_axis=0, con...]
  transfers between devices with their start and end apart: 3 -> 29, of which waited for: 2 -> 3; matrix products, arithmetic and copies ran while one was open for 10% -> 5% of each run, Pallas kernels for 0% -> 53%
where the time goes in v1:
time: 207 us; the launch traced here: 206 us
  Pallas kernels  139 us (67%)
  starting transfers between devices  44.7 us (22%)
  local copies, waits for them, and re-layouts  13 us (6%)
  waiting for transfers between devices  4.3 us (2%)
  other arithmetic  4.06 us (2%)
    pallas_call x4, Pallas kernels, mixed_group(): pl.pallas_call(functools.partial(mixed_kernel, n_col), grid_spec=pltpu.Pr...  71.8 us
    ppermute x29, starting transfers between devices, swap_with(): return lax.ppermute(value, AXES, partners(sizes, row, col, vir))  44.7 us
    pallas_call x4, Pallas kernels, final_group(): pl.pallas_call(final_kernel, grid_spec=pltpu.PrefetchScalarGridSpec(num_s...  28.2 us
    pallas_call x2, Pallas kernels, chunk_amplitudes(): pl.pallas_call(chunk_kernel, grid_spec=pltpu.PrefetchScalarGridSpec(num_s...  23.7 us
    pallas_call x1, Pallas kernels, unpack(): pl.pallas_call(functools.partial(unpack_kernel, n_col), grid_spec=pltpu.P...  10.3 us
    unnamed x68, local copies, waits for them, and re-layouts  9.21 us
    pallas_call x1, Pallas kernels, pack(): pl.pallas_call(pack_kernel, grid_spec=pltpu.PrefetchScalarGridSpec(num_sc...  4.54 us
    ppermute x29, waiting for transfers between devices, swap_with(): return lax.ppermute(value, AXES, partners(sizes, row, col, vir))  4.3 us
  transfers between devices with their start and end apart: 29, of which 3 were waited for; matrix products, arithmetic and copies ran while one was open for 5% of the time, Pallas kernels for 53%

profile of v1, /device:TPU:0, one launch (start us, length us, event | category | flops | bytes accessed | tf_op | source)
XLA Modules:
  0.0 206.1 jit_solution(4654548236947918004)
XLA Ops:
  0.6 4.5 %shard_map.118 = bf16[2,3,160,256]{3,2,1,0:T(8,128)(2,1)} custom-call(s32[4]{0:T(128)} %pad_add_fusion.5.spot_ref, s32[112]{0:T(128)} %irr_ref.3, bf16[256,256]{1,0:T(8,128)(2,1)} %constant.139.clone.turn_ref, bf16[16,3,32,448]{3,2,1,0:T(8,128)(2,1)} %bitcast.43), custom_call_target="tpu_custom_call" | custom-call | flops 400000000 | bytes 2000000 | tf_op jit(solution)/shard_map/pallas_call | solution.py:61
  5.2 3.0 %collective-permute-start.7 = (bf16[2,3,160,256]{3,2,1,0:T(8,128)(2,1)}, bf16[2,3,160,256]{3,2,1,0:T(8,128)(2,1)S(1)}, u32[]{:S(2)}, u32[]{:S(2)}) collective-permute-start(bf16[2,3,160,256]{3,2,1,0:T(8,128)(2,1)} %shard_map.118), channel_id=1, source_target_pairs={{0,8},{1,9},{2,10},{3,11},{4,12},{5,13},{6,14},{7,15},{8,0},{9,1},... | collective-permute-start | bytes 1474568 | tf_op jit(solution)/shard_map/ppermute | solution.py:428
  9.1 4.6 %collective-permute-start.9 = (bf16[1,3,160,256]{3,2,1,0:T(8,128)(2,1)S(1)}, bf16[1,3,160,256]{3,2,1,0:T(8,128)(2,1)S(1)}, u32[]{:S(2)}, u32[]{:S(2)}) collective-permute-start(bf16[1,3,160,256]{3,2,1,0:T(8,128)(2,1)S(1)} %constant_dynamic-slice_fusion.4), channel_id=1, source_target_pairs={{0,19},{1,18},{2,17},{3,16},{4,23},{5,22},{6,21},{7,20},{8,27},{9,... | collective-permute-start | bytes 737288 | tf_op jit(solution)/shard_map/ppermute | solution.py:428
  14.5 11.9 %shard_map.119 = (bf16[2,512,5376]{2,1,0:T(8,128)(2,1)}, bf16[2,2,256,128]{3,2,1,0:T(8,128)(2,1)}) custom-call(s32[4]{0:T(128)} %pad_add_fusion.5.spot_ref, bf16[16,4,16,3,2,1792]{5,4,3,2,1,0:T(2,128)(2,1)} %bitcast.41), custom_call_target="tpu_custom_call" | custom-call | flops 100000000 | bytes 23000000 | tf_op jit(solution)/shard_map/pallas_call | solution.py:155
  26.4 1.6 collective-permute-start.11
  28.5 1.6 collective-permute-start.12
  30.1 11.8 %shard_map.120 = (bf16[2,512,5376]{2,1,0:T(8,128)(2,1)}, bf16[2,2,256,128]{3,2,1,0:T(8,128)(2,1)}) custom-call(s32[4]{0:T(128)} %pad_add_fusion.5.spot_ref, bf16[16,4,16,3,2,1792]{5,4,3,2,1,0:T(2,128)(2,1)} %bitcast.42), custom_call_target="tpu_custom_call" | custom-call | flops 100000000 | bytes 23000000 | tf_op jit(solution)/shard_map/pallas_call | solution.py:155
  42.0 1.1 constant_dynamic-update-slice_fusion.9
  48.0 3.6 %copy.29 = bf16[128,16,1,2,3,64]{0,1,5,4,3,2:T(8,128)(2,1)} copy(bf16[128,16,1,2,3,64]{0,5,4,3,2,1:T(8,128)(2,1)} %param.16) | data formatting | bytes 3145728 | tf_op args[2]
  52.3 1.3 broadcast_add_fusion.pair_ref
  53.6 1.5 collective-permute-done.15
  56.3 10.3 %shard_map.121 = bf16[5376,1280]{1,0:T(8,128)(2,1)} custom-call(s32[4]{0:T(128)} %pad_add_fusion.5.spot_ref, s32[112]{0:T(128)S(1)} %copy-done.27, bf16[10,3,160,256]{3,2,1,0:T(8,128)(2,1)} %copy-done.4, bf16[10,3,160,256]{3,2,1,0:T(8,128)(2,1)} %collective-permute-done.14.far_ref), custom_call_target="tpu_custom_call" | custom-call | flops 1000000 | bytes 18000000 | tf_op jit(solution)/shard_map/pallas_call | solution.py:112
  68.5 18.1 %shard_map.122 = (f32[2,256,1024]{2,1,0:T(8,128)}, s16[2,272,256]{2,1,0:T(8,128)(2,1)}, s16[2,272,256]{2,1,0:T(8,128)(2,1)}, s16[2,272,256]{2,1,0:T(8,128)(2,1)}, s16[2,272,256]{2,1,0:T(8,128)(2,1)}) custom-call(s32[4]{0:T(128)} %pad_add_fusion.5.spot_ref, bf16[2,512,5376]{2,1,0:T(8,128)(2,1)} %get-tuple-element.343.t_ref, ...), custom_call_target="tpu_custom_call" | custom-call | flops 7200000000 | bytes 24000000 | tf_op jit(solution)/shard_map/pallas_call | solution.py:282
  87.2 1.1 collective-permute-start.18
  88.3 8.3 %collective-permute-start.19 = (s16[2,272,256]{2,1,0:T(8,128)(2,1)}, s16[2,272,256]{2,1,0:T(8,128)(2,1)S(1)}, u32[]{:S(2)}, u32[]{:S(2)}) collective-permute-start(s16[2,272,256]{2,1,0:T(8,128)(2,1)} %get-tuple-element.359), channel_id=1, source_target_pairs={{0,13},{1,12},{2,15},{3,14},{4,9},{5,8},{6,11},{7,10},{8,5},{9,4},... | collective-permute-start | bytes 835592 | tf_op jit(solution)/shard_map/ppermute | solution.py:428
  97.7 17.9 %shard_map.123 = (f32[2,256,1024]{2,1,0:T(8,128)}, s16[2,272,256]{2,1,0:T(8,128)(2,1)}, s16[2,272,256]{2,1,0:T(8,128)(2,1)}, s16[2,272,256]{2,1,0:T(8,128)(2,1)}, s16[2,272,256]{2,1,0:T(8,128)(2,1)}) custom-call(s32[4]{0:T(128)} %pad_add_fusion.5.spot_ref, bf16[2,512,5376]{2,1,0:T(8,128)(2,1)} %get-tuple-element.343.t_ref, ...), custom_call_target="tpu_custom_call" | custom-call | flops 7200000000 | bytes 24000000 | tf_op jit(solution)/shard_map/pallas_call | solution.py:282
  116.3 5.3 %collective-permute-start.23 = (s16[2,272,256]{2,1,0:T(8,128)(2,1)}, s16[2,272,256]{2,1,0:T(8,128)(2,1)S(1)}, u32[]{:S(2)}, u32[]{:S(2)}) collective-permute-start(s16[2,272,256]{2,1,0:T(8,128)(2,1)} %get-tuple-element.367), channel_id=1, source_target_pairs={{0,5},{1,4},{2,7},{3,6},{4,1},{5,0},{6,3},{7,2},{8,13},{9,12},{10,... | collective-permute-start | bytes 835592 | tf_op jit(solution)/shard_map/ppermute | solution.py:428
  121.6 1.2 collective-permute-start.24
  123.4 18.0 %shard_map.124 = (f32[2,256,1024]{2,1,0:T(8,128)}, s16[2,272,256]{2,1,0:T(8,128)(2,1)}, s16[2,272,256]{2,1,0:T(8,128)(2,1)}, s16[2,272,256]{2,1,0:T(8,128)(2,1)}, s16[2,272,256]{2,1,0:T(8,128)(2,1)}) custom-call(s32[4]{0:T(128)} %pad_add_fusion.5.spot_ref, bf16[2,512,5376]{2,1,0:T(8,128)(2,1)} %get-tuple-element.362.t_ref, ...), custom_call_target="tpu_custom_call" | custom-call | flops 7200000000 | bytes 24000000 | tf_op jit(solution)/shard_map/pallas_call | solution.py:282
  141.6 1.6 collective-permute-start.30
  143.6 1.5 collective-permute-start.27
  145.1 1.9 collective-permute-start.28
  147.9 7.1 %shard_map.125.refs_5_ = bf16[16,4,16,2,16,64]{5,4,3,2,1,0:T(8,128)(2,1)} custom-call(s32[4]{0:T(128)} %pad_add_fusion.5.spot_ref, f32[4,2,256,1]{3,2,1,0:T(8,128)} %broadcast_add_fusion.pair_ref, f32[1,1024]{1,0:T(1,128)} %add.131.slab_ref, bf16[256,256]{1,0:T(8,128)(2,1)} %constant.138.clone.turn_ref, bf16[256,256]{1,0:T(8,128)(2,1)} %constant.140.clone.swap_ref, ...), custom_call_target="tpu_custom_call" | custom-call | flops 2000000000 | bytes 10000000 | tf_op jit(solution)/shard_map/pallas_call | solution.py:374
  155.0 17.9 %shard_map.126 = (f32[2,256,1024]{2,1,0:T(8,128)}, s16[2,272,256]{2,1,0:T(8,128)(2,1)}, s16[2,272,256]{2,1,0:T(8,128)(2,1)}, s16[2,272,256]{2,1,0:T(8,128)(2,1)}, s16[2,272,256]{2,1,0:T(8,128)(2,1)}) custom-call(s32[4]{0:T(128)} %pad_add_fusion.5.spot_ref, bf16[2,512,5376]{2,1,0:T(8,128)(2,1)} %get-tuple-element.362.t_ref, ...), custom_call_target="tpu_custom_call" | custom-call | flops 7200000000 | bytes 24000000 | tf_op jit(solution)/shard_map/pallas_call | solution.py:282
  173.1 2.0 collective-permute-start.31
  175.1 1.1 collective-permute-start.32
  176.2 1.6 collective-permute-start.35
  178.5 7.1 %shard_map.127.refs_5_ = bf16[16,4,16,2,16,64]{5,4,3,2,1,0:T(8,128)(2,1)} custom-call(s32[4]{0:T(128)} %pad_add_fusion.5.spot_ref, f32[4,2,256,1]{3,2,1,0:T(8,128)} %broadcast_add_fusion.pair_ref, f32[1,1024]{1,0:T(1,128)} %add.131.slab_ref, bf16[256,256]{1,0:T(8,128)(2,1)} %constant.138.clone.turn_ref, ...), custom_call_target="tpu_custom_call", output_to_operand_aliasing={{}: (11, {})} | custom-call | flops 2000000000 | bytes 10000000 | tf_op jit(solution)/shard_map/pallas_call | solution.py:374
  186.5 2.4 %collective-permute-done.32.refs_2_ = s16[2,272,256]{2,1,0:T(8,128)(2,1)S(1)} collective-permute-done((s16[2,272,256]{2,1,0:T(8,128)(2,1)}, s16[2,272,256]{2,1,0:T(8,128)(2,1)S(1)}, u32[]{:S(2)}, u32[]{:S(2)}) %collective-permute-start.32) | collective-permute-done | bytes 278560 | tf_op jit(solution)/shard_map/ppermute | solution.py:428
  189.0 1.5 collective-permute-start.34
  191.2 7.1 %shard_map.128.refs_5_ = bf16[16,4,16,2,16,64]{5,4,3,2,1,0:T(8,128)(2,1)} custom-call(s32[4]{0:T(128)} %pad_add_fusion.5.spot_ref, f32[4,2,256,1]{3,2,1,0:T(8,128)} %broadcast_add_fusion.pair_ref, f32[1,1024]{1,0:T(1,128)} %add.131.slab_ref, bf16[256,256]{1,0:T(8,128)(2,1)} %constant.138.clone.turn_ref, ...), custom_call_target="tpu_custom_call", output_to_operand_aliasing={{}: (11, {})} | custom-call | flops 2000000000 | bytes 10000000 | tf_op jit(solution)/shard_map/pallas_call | solution.py:374
  199.1 7.1 %shard_map.129 = bf16[16,4,16,2,16,64]{5,4,3,2,1,0:T(8,128)(2,1)} custom-call(s32[4]{0:T(128)} %pad_add_fusion.5.spot_ref, f32[4,2,256,1]{3,2,1,0:T(8,128)} %broadcast_add_fusion.pair_ref, f32[1,1024]{1,0:T(1,128)} %add.131.slab_ref, bf16[256,256]{1,0:T(8,128)(2,1)} %constant.138.clone.turn_ref, ...), custom_call_target="tpu_custom_call", output_to_operand_aliasing={{}: (11, {})} | custom-call | flops 2000000000 | bytes 10000000 | tf_op jit(solution)/shard_map/pallas_call | solution.py:374
  (148 shorter events, 19.2 us)
Async XLA Ops:
  5.2 21.2 %collective-permute-start.7 = (bf16[2,3,160,256]{3,2,1,0:T(8,128)(2,1)}, bf16[2,3,160,256]{3,2,1,0:T(8,128)(2,1)S(1)}, u32[]{:S(2)}, u32[]{:S(2)}) collective-permute-start(bf16[2,3,160,256]{3,2,1,0:T(8,128)(2,1)} %shard_map.118), channel_id=1, source_target_pairs={{0,8},{1,9},{2,10},{3,11},{4,12},{5,13},{6,14},{7,15},{8,0},{9,1},... | collective-permute-start | bytes 1474568 | tf_op jit(solution)/shard_map/ppermute | solution.py:428
  9.1 17.2 %collective-permute-start.9 = (bf16[1,3,160,256]{3,2,1,0:T(8,128)(2,1)S(1)}, bf16[1,3,160,256]{3,2,1,0:T(8,128)(2,1)S(1)}, u32[]{:S(2)}, u32[]{:S(2)}) collective-permute-start(bf16[1,3,160,256]{3,2,1,0:T(8,128)(2,1)S(1)} %constant_dynamic-slice_fusion.4), channel_id=1, source_target_pairs={{0,19},{1,18},{2,17},{3,16},{4,23},{5,22},{6,21},{7,20},{8,27},{9,... | collective-permute-start | bytes 737288 | tf_op jit(solution)/shard_map/ppermute | solution.py:428
  13.7 12.7 %collective-permute-start.8 = (bf16[1,3,160,256]{3,2,1,0:T(8,128)(2,1)S(1)}, bf16[1,3,160,256]{3,2,1,0:T(8,128)(2,1)S(1)}, u32[]{:S(2)}, u32[]{:S(2)}) collective-permute-start(bf16[1,3,160,256]{3,2,1,0:T(8,128)(2,1)S(1)} %constant_dynamic-slice_fusion.4), channel_id=1, source_target_pairs={{0,3},{1,2},{2,1},{3,0},{4,7},{5,6},{6,5},{7,4},{8,11},{9,10},{10,... | collective-permute-start | bytes 737288 | tf_op jit(solution)/shard_map/ppermute | solution.py:428
  14.0 28.0 %collective-permute-start.10 = (bf16[2,3,160,256]{3,2,1,0:T(8,128)(2,1)}, bf16[2,3,160,256]{3,2,1,0:T(8,128)(2,1)}, u32[]{:S(2)}, u32[]{:S(2)}) collective-permute-start(bf16[2,3,160,256]{3,2,1,0:T(8,128)(2,1)} %shard_map.118), channel_id=1, source_target_pairs={{0,16},{1,17},{2,18},{3,19},{4,20},{5,21},{6,22},{7,23},{8,24},{9,... | collective-permute-start | bytes 1474568 | tf_op jit(solution)/shard_map/ppermute | solution.py:428
  26.4 15.6 %collective-permute-start.11 = (bf16[2,3,160,256]{3,2,1,0:T(8,128)(2,1)S(1)}, bf16[2,3,160,256]{3,2,1,0:T(8,128)(2,1)}, u32[]{:S(2)}, u32[]{:S(2)}) collective-permute-start(bf16[2,3,160,256]{3,2,1,0:T(8,128)(2,1)S(1)} %collective-permute-done.7), channel_id=1, source_target_pairs={{0,16},{1,17},{2,18},{3,19},{4,20},{5,21},{6,22},{7,23},{8,24},{9,... | collective-permute-start | bytes 1474568 | tf_op jit(solution)/shard_map/ppermute | solution.py:428
  28.0 14.0 %collective-permute-start.13 = (bf16[2,2,256,128]{3,2,1,0:T(8,128)(2,1)}, bf16[2,2,256,128]{3,2,1,0:T(8,128)(2,1)}, u32[]{:S(2)}, u32[]{:S(2)}) collective-permute-start(bf16[2,2,256,128]{3,2,1,0:T(8,128)(2,1)} %get-tuple-element.333), channel_id=1, source_target_pairs={{0,8},{1,9},{2,10},{3,11},{4,12},{5,13},{6,14},{7,15},{8,0},{9,1},... | collective-permute-start | bytes 786440 | tf_op jit(solution)/shard_map/ppermute | solution.py:428
  28.5 13.5 %collective-permute-start.12 = (bf16[1,3,160,256]{3,2,1,0:T(8,128)(2,1)S(1)}, bf16[1,3,160,256]{3,2,1,0:T(8,128)(2,1)S(1)}, u32[]{:S(2)}, u32[]{:S(2)}) collective-permute-start(bf16[1,3,160,256]{3,2,1,0:T(8,128)(2,1)S(1)} %broadcast_select_fusion.1), channel_id=1, source_target_pairs={{0,8},{1,9},{2,10},{3,11},{4,12},{5,13},{6,14},{7,15},{8,0},{9,1},... | collective-permute-start | bytes 737288 | tf_op jit(solution)/shard_map/ppermute | solution.py:428
  44.3 10.8 %collective-permute-start.14 = (bf16[10,3,160,256]{3,2,1,0:T(8,128)(2,1)S(1)}, bf16[10,3,160,256]{3,2,1,0:T(8,128)(2,1)}, u32[]{:S(2)}, u32[]{:S(2)}) collective-permute-start(bf16[10,3,160,256]{3,2,1,0:T(8,128)(2,1)S(1)} %constant_dynamic-update-slice_fusion.6.near_ref), channel_id=1, source_target_pairs={{0,4},{1,5},{2,6},{3,7},{4,0},{5,1},{6,2},{7,3},{8,12},{9,13},{10,... | collective-permute-start | bytes 7372808 | tf_op jit(solution)/shard_map/ppermute | solution.py:428
  46.4 8.7 %collective-permute-start.15 = (bf16[2,2,256,128]{3,2,1,0:T(8,128)(2,1)S(1)}, bf16[2,2,256,128]{3,2,1,0:T(8,128)(2,1)S(1)}, u32[]{:S(2)}, u32[]{:S(2)}) collective-permute-start(bf16[2,2,256,128]{3,2,1,0:T(8,128)(2,1)S(1)} %copy-done.26), channel_id=1, source_target_pairs={{0,8},{1,9},{2,10},{3,11},{4,12},{5,13},{6,14},{7,15},{8,0},{9,1},... | collective-permute-start | bytes 786440 | tf_op jit(solution)/shard_map/ppermute | solution.py:428
  56.2 10.4 %collective-permute-start.16 = (bf16[4,2,2,256,128]{4,3,2,1,0:T(8,128)(2,1)S(1)}, bf16[4,2,2,256,128]{4,3,2,1,0:T(8,128)(2,1)S(1)}, u32[]{:S(2)}, u32[]{:S(2)}) collective-permute-start(bf16[4,2,2,256,128]{4,3,2,1,0:T(8,128)(2,1)S(1)} %pad_maximum_fusion.refs_0_.refs_2_), channel_id=1, source_target_pairs={{0,4},{1,5},{2,6},{3,7},{4,0},{5,1},{6,2},{7,3},{8,12},{9,13},{10,... | collective-permute-start | bytes 3145736 | tf_op jit(solution)/shard_map/ppermute | solution.py:428
  86.5 29.1 %collective-permute-start.17 = (s16[2,272,256]{2,1,0:T(8,128)(2,1)}, s16[2,272,256]{2,1,0:T(8,128)(2,1)S(1)}, u32[]{:S(2)}, u32[]{:S(2)}) collective-permute-start(s16[2,272,256]{2,1,0:T(8,128)(2,1)} %get-tuple-element.357), channel_id=1, source_target_pairs={{0,12},{1,13},{2,14},{3,15},{4,8},{5,9},{6,10},{7,11},{8,4},{9,5},... | collective-permute-start | bytes 835592 | tf_op jit(solution)/shard_map/ppermute | solution.py:428
  87.2 29.1 %collective-permute-start.18 = (s16[2,272,256]{2,1,0:T(8,128)(2,1)}, s16[2,272,256]{2,1,0:T(8,128)(2,1)S(1)}, u32[]{:S(2)}, u32[]{:S(2)}) collective-permute-start(s16[2,272,256]{2,1,0:T(8,128)(2,1)} %get-tuple-element.358), channel_id=1, source_target_pairs={{0,28},{1,29},{2,30},{3,31},{4,24},{5,25},{6,26},{7,27},{8,20},{9,... | collective-permute-start | bytes 835592 | tf_op jit(solution)/shard_map/ppermute | solution.py:428
  88.3 33.3 %collective-permute-start.19 = (s16[2,272,256]{2,1,0:T(8,128)(2,1)}, s16[2,272,256]{2,1,0:T(8,128)(2,1)S(1)}, u32[]{:S(2)}, u32[]{:S(2)}) collective-permute-start(s16[2,272,256]{2,1,0:T(8,128)(2,1)} %get-tuple-element.359), channel_id=1, source_target_pairs={{0,13},{1,12},{2,15},{3,14},{4,9},{5,8},{6,11},{7,10},{8,5},{9,4},... | collective-permute-start | bytes 835592 | tf_op jit(solution)/shard_map/ppermute | solution.py:428
  96.6 26.1 %collective-permute-start.20 = (s16[2,272,256]{2,1,0:T(8,128)(2,1)}, s16[2,272,256]{2,1,0:T(8,128)(2,1)S(1)}, u32[]{:S(2)}, u32[]{:S(2)}) collective-permute-start(s16[2,272,256]{2,1,0:T(8,128)(2,1)} %get-tuple-element.360), channel_id=1, source_target_pairs={{0,14},{1,15},{2,12},{3,13},{4,10},{5,11},{6,8},{7,9},{8,6},{9,7},... | collective-permute-start | bytes 835592 | tf_op jit(solution)/shard_map/ppermute | solution.py:428
  115.6 25.9 %collective-permute-start.21 = (s16[2,272,256]{2,1,0:T(8,128)(2,1)}, s16[2,272,256]{2,1,0:T(8,128)(2,1)S(1)}, u32[]{:S(2)}, u32[]{:S(2)}) collective-permute-start(s16[2,272,256]{2,1,0:T(8,128)(2,1)} %get-tuple-element.365), channel_id=1, source_target_pairs={{0,4},{1,5},{2,6},{3,7},{4,0},{5,1},{6,2},{7,3},{8,12},{9,13},{10,... | collective-permute-start | bytes 835592 | tf_op jit(solution)/shard_map/ppermute | solution.py:428
  115.7 25.7 %copy-start.14 = (s16[2,272,256]{2,1,0:T(8,128)(2,1)}, s16[2,272,256]{2,1,0:T(8,128)(2,1)S(1)}, u32[]{:S(2)}) copy-start(s16[2,272,256]{2,1,0:T(8,128)(2,1)S(1)} %collective-permute-done.17.refs_0_) | copy-start | bytes 835588
  115.7 25.8 %collective-permute-start.22 = (s16[2,272,256]{2,1,0:T(8,128)(2,1)}, s16[2,272,256]{2,1,0:T(8,128)(2,1)S(1)}, u32[]{:S(2)}, u32[]{:S(2)}) collective-permute-start(s16[2,272,256]{2,1,0:T(8,128)(2,1)} %get-tuple-element.366), channel_id=1, source_target_pairs={{0,20},{1,21},{2,22},{3,23},{4,16},{5,17},{6,18},{7,19},{8,28},{9,... | collective-permute-start | bytes 835592 | tf_op jit(solution)/shard_map/ppermute | solution.py:428
  116.3 25.1 %copy-start.15 = (s16[2,272,256]{2,1,0:T(8,128)(2,1)}, s16[2,272,256]{2,1,0:T(8,128)(2,1)S(1)}, u32[]{:S(2)}) copy-start(s16[2,272,256]{2,1,0:T(8,128)(2,1)S(1)} %collective-permute-done.18.refs_3_) | copy-start | bytes 835588
  116.3 25.2 %collective-permute-start.23 = (s16[2,272,256]{2,1,0:T(8,128)(2,1)}, s16[2,272,256]{2,1,0:T(8,128)(2,1)S(1)}, u32[]{:S(2)}, u32[]{:S(2)}) collective-permute-start(s16[2,272,256]{2,1,0:T(8,128)(2,1)} %get-tuple-element.367), channel_id=1, source_target_pairs={{0,5},{1,4},{2,7},{3,6},{4,1},{5,0},{6,3},{7,2},{8,13},{9,12},{10,... | collective-permute-start | bytes 835592 | tf_op jit(solution)/shard_map/ppermute | solution.py:428
  121.6 19.8 %copy-start.6 = (s16[2,272,256]{2,1,0:T(8,128)(2,1)}, s16[2,272,256]{2,1,0:T(8,128)(2,1)S(1)}, u32[]{:S(2)}) copy-start(s16[2,272,256]{2,1,0:T(8,128)(2,1)S(1)} %collective-permute-done.19.refs_1_) | copy-start | bytes 835588
  121.6 19.9 %collective-permute-start.24 = (s16[2,272,256]{2,1,0:T(8,128)(2,1)}, s16[2,272,256]{2,1,0:T(8,128)(2,1)S(1)}, u32[]{:S(2)}, u32[]{:S(2)}) collective-permute-start(s16[2,272,256]{2,1,0:T(8,128)(2,1)} %get-tuple-element.368), channel_id=1, source_target_pairs={{0,6},{1,7},{2,4},{3,5},{4,2},{5,3},{6,0},{7,1},{8,14},{9,15},{10,... | collective-permute-start | bytes 835592 | tf_op jit(solution)/shard_map/ppermute | solution.py:428
  122.8 24.2 %collective-permute-start.25 = (s16[2,272,256]{2,1,0:T(8,128)(2,1)S(1)}, s16[2,272,256]{2,1,0:T(8,128)(2,1)S(1)}, u32[]{:S(2)}, u32[]{:S(2)}) collective-permute-start(s16[2,272,256]{2,1,0:T(8,128)(2,1)S(1)} %pad_add_fusion.1), channel_id=1, source_target_pairs={{0,16},{1,17},{2,18},{3,19},{4,20},{5,21},{6,22},{7,23},{8,24},{9,... | collective-permute-start | bytes 835592 | tf_op jit(solution)/shard_map/ppermute | solution.py:428
  141.6 36.2 %collective-permute-start.30 = (s16[2,272,256]{2,1,0:T(8,128)(2,1)S(1)}, s16[2,272,256]{2,1,0:T(8,128)(2,1)S(1)}, u32[]{:S(2)}, u32[]{:S(2)}) collective-permute-start(s16[2,272,256]{2,1,0:T(8,128)(2,1)S(1)} %pad_add_fusion.2), channel_id=1, source_target_pairs={{0,16},{1,17},{2,18},{3,19},{4,20},{5,21},{6,22},{7,23},{8,24},{9,... | collective-permute-start | bytes 835592 | tf_op jit(solution)/shard_map/ppermute | solution.py:428
  143.2 29.8 %collective-permute-start.26 = (s16[2,272,256]{2,1,0:T(8,128)(2,1)}, s16[2,272,256]{2,1,0:T(8,128)(2,1)S(1)}, u32[]{:S(2)}, u32[]{:S(2)}) collective-permute-start(s16[2,272,256]{2,1,0:T(8,128)(2,1)} %get-tuple-element.380), channel_id=1, source_target_pairs={{0,8},{1,9},{2,10},{3,11},{4,12},{5,13},{6,14},{7,15},{8,0},{9,1},... | collective-permute-start | bytes 835592 | tf_op jit(solution)/shard_map/ppermute | solution.py:428
  143.6 29.3 %collective-permute-start.27 = (s16[2,272,256]{2,1,0:T(8,128)(2,1)}, s16[2,272,256]{2,1,0:T(8,128)(2,1)S(1)}, u32[]{:S(2)}, u32[]{:S(2)}) collective-permute-start(s16[2,272,256]{2,1,0:T(8,128)(2,1)} %get-tuple-element.381), channel_id=1, source_target_pairs={{0,24},{1,25},{2,26},{3,27},{4,28},{5,29},{6,30},{7,31},{8,16},{9,... | collective-permute-start | bytes 835592 | tf_op jit(solution)/shard_map/ppermute | solution.py:428
  145.1 27.9 %collective-permute-start.28 = (s16[2,272,256]{2,1,0:T(8,128)(2,1)}, s16[2,272,256]{2,1,0:T(8,128)(2,1)S(1)}, u32[]{:S(2)}, u32[]{:S(2)}) collective-permute-start(s16[2,272,256]{2,1,0:T(8,128)(2,1)} %get-tuple-element.382), channel_id=1, source_target_pairs={{0,9},{1,8},{2,11},{3,10},{4,13},{5,12},{6,15},{7,14},{8,1},{9,0},... | collective-permute-start | bytes 835592 | tf_op jit(solution)/shard_map/ppermute | solution.py:428
  147.0 26.0 %collective-permute-start.29 = (s16[2,272,256]{2,1,0:T(8,128)(2,1)}, s16[2,272,256]{2,1,0:T(8,128)(2,1)S(1)}, u32[]{:S(2)}, u32[]{:S(2)}) collective-permute-start(s16[2,272,256]{2,1,0:T(8,128)(2,1)} %get-tuple-element.383), channel_id=1, source_target_pairs={{0,10},{1,11},{2,8},{3,9},{4,14},{5,15},{6,12},{7,13},{8,2},{9,3},... | collective-permute-start | bytes 835592 | tf_op jit(solution)/shard_map/ppermute | solution.py:428
  173.1 13.4 %collective-permute-start.31 = (s16[2,272,256]{2,1,0:T(8,128)(2,1)}, s16[2,272,256]{2,1,0:T(8,128)(2,1)S(1)}, u32[]{:S(2)}, u32[]{:S(2)}) collective-permute-start(s16[2,272,256]{2,1,0:T(8,128)(2,1)} %get-tuple-element.392), channel_id=1, source_target_pairs={{0,1},{1,0},{2,3},{3,2},{4,5},{5,4},{6,7},{7,6},{8,9},{9,8},{10,11... | collective-permute-start | bytes 835592 | tf_op jit(solution)/shard_map/ppermute | solution.py:428
  175.1 13.8 %collective-permute-start.32 = (s16[2,272,256]{2,1,0:T(8,128)(2,1)}, s16[2,272,256]{2,1,0:T(8,128)(2,1)S(1)}, u32[]{:S(2)}, u32[]{:S(2)}) collective-permute-start(s16[2,272,256]{2,1,0:T(8,128)(2,1)} %get-tuple-element.393), channel_id=1, source_target_pairs={{0,2},{1,3},{2,0},{3,1},{4,6},{5,7},{6,4},{7,5},{8,10},{9,11},{10,... | collective-permute-start | bytes 835592 | tf_op jit(solution)/shard_map/ppermute | solution.py:428
  176.2 14.3 %collective-permute-start.35 = (s16[2,272,256]{2,1,0:T(8,128)(2,1)S(1)}, s16[2,272,256]{2,1,0:T(8,128)(2,1)S(1)}, u32[]{:S(2)}, u32[]{:S(2)}) collective-permute-start(s16[2,272,256]{2,1,0:T(8,128)(2,1)S(1)} %pad_add_fusion.4), channel_id=1, source_target_pairs={{0,16},{1,17},{2,18},{3,19},{4,20},{5,21},{6,22},{7,23},{8,24},{9,... | collective-permute-start | bytes 835592 | tf_op jit(solution)/shard_map/ppermute | solution.py:428
  185.6 12.6 %collective-permute-start.33 = (s16[2,272,256]{2,1,0:T(8,128)(2,1)S(1)}, s16[2,272,256]{2,1,0:T(8,128)(2,1)S(1)}, u32[]{:S(2)}, u32[]{:S(2)}) collective-permute-start(s16[2,272,256]{2,1,0:T(8,128)(2,1)S(1)} %copy-done.31), channel_id=1, source_target_pairs={{0,16},{1,17},{2,18},{3,19},{4,20},{5,21},{6,22},{7,23},{8,24},{9,... | collective-permute-start | bytes 835592 | tf_op jit(solution)/shard_map/ppermute | solution.py:428
  189.0 9.3 %collective-permute-start.34 = (s16[2,272,256]{2,1,0:T(8,128)(2,1)S(1)}, s16[2,272,256]{2,1,0:T(8,128)(2,1)S(1)}, u32[]{:S(2)}, u32[]{:S(2)}) collective-permute-start(s16[2,272,256]{2,1,0:T(8,128)(2,1)S(1)} %pad_add_fusion.3), channel_id=1, source_target_pairs={{0,16},{1,17},{2,18},{3,19},{4,20},{5,21},{6,22},{7,23},{8,24},{9,... | collective-permute-start | bytes 835592 | tf_op jit(solution)/shard_map/ppermute | solution.py:428
  (28 other events, 229.4 us)

commit v2 on v1

--- a/solution.py
+++ b/solution.py
@@ -195,7 +195,7 @@
 
 def mixed_kernel(n_col, spot_ref, t_ref, v_ref, w_ref, order_ref, *refs):
     parts, refs = refs[:n_col], refs[n_col:]
-    u_ref, near0_ref, near1_ref, one_ref, two_ref, acc, zs, ints, slabs = refs
+    u_ref, near_ref, one_ref, two_ref, acc, zs, ints, slabs = refs
     step = pl.program_id(0)
     rows = 2 * WIDE
 
@@ -232,7 +232,7 @@
             most = jnp.maximum(jnp.max(jnp.abs(value), axis=0, keepdims=True), 1e-30)
             grade = jnp.ceil(jnp.log2(most) * GRAIN)
             scale = TOP * jnp.exp2(-grade / GRAIN)
-            whole = jnp.floor(value * scale + 0.5).astype(jnp.int32).astype(jnp.int16)
+            whole = ((value * scale + 32768.5).astype(jnp.int32) - 32768).astype(jnp.int16)
             grades = jnp.broadcast_to(grade, (16, WIDE)).astype(jnp.int32).astype(jnp.int16)
             ints[dr, :WIDE, :] = whole
             ints[dr, WIDE:, :] = grades
@@ -260,17 +260,19 @@
             outs[dr][...] = ints[dr]
 
     for n, outs in (
-        (1, (near0_ref.at[1], near1_ref.at[1])),
-        (2, (near0_ref.at[0], near1_ref.at[0])),
+        (1, (near_ref.at[0, 1], near_ref.at[1, 1])),
+        (2, (near_ref.at[0, 0], near_ref.at[1, 0])),
         (3, (one_ref.at[0], one_ref.at[1])),
         (4, (two_ref.at[0], two_ref.at[1])),
     ):
         pl.when(step == n)(functools.partial(send, outs))
 
 
-def mixed_group(dc, spot, t, at, v, w, order, near, far, n_col):
+def mixed_group(dc, spot, t, at, v, w, order, slabs, slabs_far, n_col):
     ints = jax.ShapeDtypeStruct((2, WIDE + 16, WIDE), jnp.int16)
     ints_spec = pl.BlockSpec(ints.shape, lambda n, spot: (0, 0, 0))
+    near = jax.ShapeDtypeStruct((2,) + ints.shape, jnp.int16)
+    near_spec = pl.BlockSpec(near.shape, lambda n, spot: (0, 0, 0, 0))
 
     def slab_spec(other):
         group = dc ^ other
@@ -297,7 +299,7 @@
             out_specs=[
                 pl.BlockSpec((2, WIDE, WIDE), lambda n, spot: (0, 0, jnp.clip(n - 2, 0, 3)))
             ]
-            + [ints_spec] * 4,
+            + [near_spec, ints_spec, ints_spec],
             scratch_shapes=[
                 pltpu.VMEM((2, 2 * WIDE, LANES), F32),
                 pltpu.VMEM((2, 2 * WIDE, LANES), F32),
@@ -305,10 +307,10 @@
                 pltpu.VMEM((2, CW * NO, WIDE), BF),
             ],
         ),
-        out_shape=[jax.ShapeDtypeStruct((2, WIDE, 4 * WIDE), F32)] + [ints] * 4,
+        out_shape=[jax.ShapeDtypeStruct((2, WIDE, 4 * WIDE), F32), near, ints, ints],
         compiler_params=PARAMS,
         cost_estimate=cost(7.2e9, 24e6),
-    )(spot, t, v, w, order, *([near, far] * 2))
+    )(spot, t, v, w, order, *([slabs, slabs_far] * 2))
 
 
 def trade_rows(x):
@@ -326,18 +328,21 @@
     return x
 
 
-def final_kernel(spot_ref, pair_ref, slab_ref, turn_ref, swap_ref, u_ref, *refs):
-    got, (out_ref, ints, incs, os) = refs[:5], refs[-4:]
+def final_kernel(split, dc, n_col, spot_ref, occ_ref, vir_ref, turn_ref, swap_ref, u_ref, *refs):
+    got, (out_ref, ints, incs, os) = refs[:-4], refs[-4:]
     step = pl.program_id(0)
     for dr in range(2):
 
         @pl.when(step == dr)
         def _(dr=dr):
             if dr == 0:
-                near, one, two = got[0], got[1].at[0], got[2].at[0]
+                parts = [got[0].at[0, 0], got[1].at[0], got[2].at[0], got[0].at[0, 1]]
+            elif split:
+                parts = [got[3].at[0], got[4].at[0], got[4].at[1], got[3].at[1]]
             else:
-                near, one, two = got[3], got[4].at[0], got[4].at[1]
-            ints[0], ints[1], ints[2], ints[3] = near[0], one[...], two[...], near[1]
+                parts = [got[3].at[0], got[3].at[2], got[3].at[3], got[3].at[1]]
+            for t, part in enumerate(parts):
+                ints[t] = part[...]
 
     own = u_ref[0]
     high = own.astype(BF)
@@ -346,13 +351,31 @@
     both = jnp.dot(turn_ref[...], both, preferred_element_type=F32).astype(BF)
     both = jnp.concatenate([both[:, i * WIDE : (i + 1) * WIDE] for i in range(8)], axis=0)
     both = jnp.dot(both, swap_ref[...], preferred_element_type=F32)
-    pair = pair_ref[0, 0]
+    m, s = spot_ref[1] ^ dc, spot_ref[0] ^ step
+    row = lax.broadcasted_iota(jnp.int32, (8, LANES), 0)
+    first = []
+    for q_half in range(2):
+        energy = jnp.zeros((8, LANES), F32)
+        for k in range(8):
+            energy = jnp.where(row == k, occ_ref[((q_half * 8 + k) * n_col + m) * 2 + spot_ref[0]], energy)
+        first.append(energy)
+    pair = jnp.concatenate(
+        [first[g % 2] + occ_ref[((g // 2) * n_col + spot_ref[1]) * 2 + s] for g in range(32)], axis=0
+    )
+    pair = jnp.concatenate([pair, pair], axis=1)
+    lane = lax.broadcasted_iota(jnp.int32, (1, WIDE), 1)
+    energy_a = jnp.zeros((1, WIDE), F32)
+    for p in range(VBLK):
+        energy_a = jnp.where(lane // VBLK == p, vir_ref[spot_ref[2] * VBLK + NAMED[p]], energy_a)
     for t in range(4):
+        energy_b = jnp.zeros((1, WIDE), F32)
+        for b in range(VBLK):
+            energy_b = jnp.where(lane % VBLK == b, vir_ref[(spot_ref[2] ^ t) * VBLK + b], energy_b)
         mine = both[t * WIDE : (t + 1) * WIDE] + both[(t + 4) * WIDE : (t + 5) * WIDE]
         grade = ints[t, WIDE : WIDE + 16, :].astype(jnp.int32).astype(F32)[:1]
         scale = jnp.exp2(grade / GRAIN) / TOP
         mirror = ints[t, :WIDE, :].astype(jnp.int32).astype(F32) * scale
-        incs[t] = (mine + mirror) / (pair - slab_ref[:, t * WIDE : (t + 1) * WIDE])
+        incs[t] = (mine + mirror) / (pair - energy_a - energy_b)
     for h in range(16):
         for q_half in range(2):
             rows = slice(h * 16 + q_half * 8, h * 16 + q_half * 8 + 8)
@@ -367,26 +390,26 @@
     out_ref[...] = os[...][:, :SA].astype(BF).reshape(out_ref.shape)
 
 
-def final_group(dc, spot, pair, slab, turn, swap, u, got, out):
-    near_spec = pl.BlockSpec((2, WIDE + 16, WIDE), lambda i, spot: (0, 0, 0))
-    far_spec = pl.BlockSpec((1, WIDE + 16, WIDE), lambda i, spot: (0, 0, 0))
+def final_group(dc, n_col, spot, occ, vir, turn, swap, u, got, out):
+    split = len(got) == 5
+    got_specs = [pl.BlockSpec((1, 2, WIDE + 16, WIDE), lambda i, spot, *_: (0, 0, 0, 0))]
+    got_specs += [pl.BlockSpec((1, WIDE + 16, WIDE), lambda i, spot, *_: (0, 0, 0))] * 2
+    got_specs += [pl.BlockSpec(x.shape, lambda i, spot, *_: (0, 0, 0)) for x in got[3:]]
     more = [] if out is None else [out]
     return pl.pallas_call(
-        final_kernel,
+        functools.partial(final_kernel, split, dc, n_col),
         grid_spec=pltpu.PrefetchScalarGridSpec(
-            num_scalar_prefetch=1,
+            num_scalar_prefetch=3,
             grid=(2,),
             in_specs=[
-                pl.BlockSpec((1, 1, WIDE, 1), lambda i, spot: (spot[1] ^ dc, i ^ spot[0], 0, 0)),
-                pl.BlockSpec(slab.shape, lambda i, spot: (0, 0)),
-                pl.BlockSpec(turn.shape, lambda i, spot: (0, 0)),
-                pl.BlockSpec(swap.shape, lambda i, spot: (0, 0)),
-                pl.BlockSpec((1, WIDE, 4 * WIDE), lambda i, spot: (i ^ spot[0], 0, 0)),
+                pl.BlockSpec(turn.shape, lambda i, spot, *_: (0, 0)),
+                pl.BlockSpec(swap.shape, lambda i, spot, *_: (0, 0)),
+                pl.BlockSpec((1, WIDE, 4 * WIDE), lambda i, spot, *_: (i ^ spot[0], 0, 0)),
             ]
-            + [near_spec, far_spec, far_spec, near_spec, near_spec]
+            + got_specs
             + [ANY] * len(more),
             out_specs=pl.BlockSpec(
-                (16, 1, 16, 1, VBLK, SA), lambda i, spot: (0, spot[1] ^ dc, 0, i ^ spot[0], 0, 0)
+                (16, 1, 16, 1, VBLK, SA), lambda i, spot, *_: (0, spot[1] ^ dc, 0, i ^ spot[0], 0, 0)
             ),
             scratch_shapes=[
                 pltpu.VMEM((4, WIDE + 16, WIDE), jnp.int16),
@@ -395,10 +418,10 @@
             ],
         ),
         out_shape=jax.ShapeDtypeStruct((16, 4, 16, 2, VBLK, SA), BF),
-        input_output_aliases={11: 0} if more else {},
+        input_output_aliases={6 + len(got): 0} if more else {},
         compiler_params=PARAMS,
         cost_estimate=cost(2e9, 10e6),
-    )(spot, pair, slab, turn, swap, u, *got, *more)
+    )(spot, occ, vir, turn, swap, u, *got, *more)
 
 
 def partners(sizes, row, col, vir):
@@ -456,15 +479,6 @@
     every = irreps.reshape(1, n_col, -1) == jnp.arange(8, dtype=irreps.dtype)[:, None, None]
     fullest = jnp.max(jnp.sum(every.astype(jnp.int32), axis=-1))
 
-    energy_i = lax.dynamic_index_in_dim(occ_energy.reshape(groups, n_col, n_row), row_pos, 2, False)
-    energy_j = lax.dynamic_index_in_dim(occ_energy.reshape(occ_h, n_col, n_row), col_pos, 1, False)
-    pair = energy_i.T[:, None, None, :] + energy_j.T[None, :, :, None]
-    pair = pair.reshape(n_col, n_row, occ_h * groups, 1)
-    energies = vir_energy.reshape(n_vir, VBLK)
-    energy_a = lax.dynamic_index_in_dim(energies, vir_pos, 0, False)[named]
-    energy_b = jnp.take(energies, vir_pos ^ jnp.arange(n_vir), axis=0)
-    slab_sum = (energy_a[None, :, None] + energy_b[:, None, :]).reshape(1, n_vir * WIDE)
-
     mine = pack(spot, irreps, by_b, shard)
     spot, mine = later(spot, mine)
 
@@ -487,7 +501,7 @@
     near, far = gather(mine, hold, hold_second)
     spot, slabs = state["spot"], state["slabs"]
     holes = jnp.transpose(hole_integrals.reshape(NO, occ_h, n_row, CW, SA), (2, 3, 4, 1, 0))
-    spot, near, holes, pair, slab_sum, fullest = later(spot, near, holes, pair, slab_sum, fullest)
+    spot, near, holes, fullest = later(spot, near, holes, fullest)
     rows_of = [(first, 0), (first, 1), (state["second"], 0), (state["second"], 1)]
     spot, far, slabs[3] = later(spot, far, slabs[3])
     slabs = jnp.stack(slabs)
@@ -516,38 +530,44 @@
 
     def sum_group(chunk, spot, out):
         dc, u, got = chunk
-        return final_group(dc, spot, pair, slab_sum, flip, swap, u, got, out)
+        return final_group(dc, n_col, spot, occ_energy, vir_energy, flip, swap, u, got, out)
 
     def arrive(chunk, spot, *waited):
         held = [chunk[2][name] for name in waited]
         spot, held = lax.optimization_barrier((spot, held))
         chunk[2].update(zip(waited, held))
-        far = chunk[2]["far"]
-        on = swap_with(jnp.stack([piece[1] for piece in far]), 1, 0, 0)
-        chunk[2] = [chunk[2]["near"][0], *far, chunk[2]["near"][1], on]
+        near, one, two = chunk[2]["near"], chunk[2]["one"], chunk[2]["two"]
+        if "beyond" in chunk[2]:
+            rest = [chunk[2]["beyond"], swap_with(jnp.stack([one[1], two[1]]), 1, 0, 0)]
+        else:
+            rest = [swap_with(jnp.concatenate([near[1], one[1:], two[1:]], axis=0), 1, 0, 0)]
+        chunk[2] = [near, one, two, *rest]
         return spot
 
     out = None
     chunks = []
     for turn, dc in enumerate((3, 1, 2, 0)):
         if turn >= 2:
-            spot = arrive(chunks[turn - 2], spot, "near", "far")
+            spot = arrive(chunks[turn - 2], spot, "near", "one", "two")
         if turn == 3:
             out = sum_group(chunks[0], spot, out)
             spot, out = lax.optimization_barrier((spot, out))
-        u, near0, near1, one, two = mixed_group(
+        u, near, one, two = mixed_group(
             dc, spot, *rows_of[turn], dense, holes, order, slabs, slabs_far, n_col
         )
         sent = {
-            "near": [swap_with(near0, 0, dc, 0), swap_with(near1, 1, dc, 0)],
-            "far": [swap_with(one, 0, dc, 1), swap_with(two, 0, dc, 2)],
+            "near": swap_with(near, 0, dc, 0),
+            "one": swap_with(one, 0, dc, 1),
+            "two": swap_with(two, 0, dc, 2),
         }
+        if dc == 0:
+            sent["beyond"] = swap_with(near[1], 1, 0, 0)
         spot, u = lax.optimization_barrier((spot, u))
         chunks.append([dc, u, sent])
-    spot = arrive(chunks[2], spot, "near", "far")
+    spot = arrive(chunks[2], spot, "near", "one", "two")
     out = sum_group(chunks[1], spot, out)
     spot, out = lax.optimization_barrier((spot, out))
-    spot = arrive(chunks[3], spot, "far")
+    spot = arrive(chunks[3], spot, "one", "two")
     for turn in (2, 3):
         out = sum_group(chunks[turn], spot, out)
     return out.reshape(occ_a, 1, occ_h, 1, n_row, VBLK, SA)

time: 207 us -> 205 us (level)
  waiting for transfers between devices: 4.3 us -> 11.9 us
  starting transfers between devices: 44.7 us -> 38.2 us
    ppermute x29 -> x26, waiting for transfers between devices: 4.3 us -> 11.9 us  [swap_with(): return lax.ppermute(value, AXES, partners(sizes, row, col, vir))]
    ppermute x29 -> x26, starting transfers between devices: 44.7 us -> 38.2 us  [swap_with(): return lax.ppermute(value, AXES, partners(sizes, row, col, vir))]
    unnamed x68 -> x54, local copies, waits for them, and re-layouts: 9.21 us -> 10.1 us
  transfers between devices with their start and end apart: 29 -> 26, of which waited for: 3 -> 6; matrix products, arithmetic and copies ran while one was open for 5% -> 3% of each run, Pallas kernels for 53% -> 53%
where the time goes in v2:
time: 205 us; the launch traced here: 204 us
  Pallas kernels  138 us (67%)
  starting transfers between devices  38.2 us (19%)
  waiting for transfers between devices  11.9 us (6%)
  local copies, waits for them, and re-layouts  11.4 us (6%)
  other arithmetic  2.8 us (1%)
    pallas_call x4, Pallas kernels, mixed_group(): pl.pallas_call(functools.partial(mixed_kernel, n_col), grid_spec=pltpu.Pr...  71.8 us
    ppermute x26, starting transfers between devices, swap_with(): return lax.ppermute(value, AXES, partners(sizes, row, col, vir))  38.2 us
    pallas_call x4, Pallas kernels, final_group(): pl.pallas_call(functools.partial(final_kernel, split, dc, n_col), grid_sp...  28.1 us
    pallas_call x2, Pallas kernels, chunk_amplitudes(): pl.pallas_call(chunk_kernel, grid_spec=pltpu.PrefetchScalarGridSpec(num_s...  23.6 us
    ppermute x26, waiting for transfers between devices, swap_with(): return lax.ppermute(value, AXES, partners(sizes, row, col, vir))  11.9 us
    unnamed x54, local copies, waits for them, and re-layouts  10.1 us
    pallas_call x1, Pallas kernels, unpack(): pl.pallas_call(functools.partial(unpack_kernel, n_col), grid_spec=pltpu.P...  10.1 us
    pallas_call x1, Pallas kernels, pack(): pl.pallas_call(pack_kernel, grid_spec=pltpu.PrefetchScalarGridSpec(num_sc...  4.54 us
  transfers between devices with their start and end apart: 26, of which 6 were waited for; matrix products, arithmetic and copies ran while one was open for 3% of the time, Pallas kernels for 53%

profile of v2, /device:TPU:0, one launch (start us, length us, event | category | flops | bytes accessed | tf_op | source)
XLA Modules:
  0.0 203.8 jit_solution(10090912453017441087)
XLA Ops:
  0.7 4.5 %shard_map.100 = bf16[2,3,160,256]{3,2,1,0:T(8,128)(2,1)} custom-call(s32[4]{0:T(128)} %pad_add_fusion.5.spot_ref, s32[112]{0:T(128)} %irr_ref.3, bf16[256,256]{1,0:T(8,128)(2,1)} %constant.107.clone.turn_ref, bf16[16,3,32,448]{3,2,1,0:T(8,128)(2,1)} %bitcast.41), custom_call_target="tpu_custom_call" | custom-call | flops 400000000 | bytes 2000000 | tf_op jit(solution)/shard_map/pallas_call | solution.py:61
  5.2 3.0 %collective-permute-start.7 = (bf16[2,3,160,256]{3,2,1,0:T(8,128)(2,1)}, bf16[2,3,160,256]{3,2,1,0:T(8,128)(2,1)S(1)}, u32[]{:S(2)}, u32[]{:S(2)}) collective-permute-start(bf16[2,3,160,256]{3,2,1,0:T(8,128)(2,1)} %shard_map.100), channel_id=1, source_target_pairs={{0,8},{1,9},{2,10},{3,11},{4,12},{5,13},{6,14},{7,15},{8,0},{9,1},... | collective-permute-start | bytes 1474568 | tf_op jit(solution)/shard_map/ppermute | solution.py:451
  9.2 4.6 %collective-permute-start.9 = (bf16[1,3,160,256]{3,2,1,0:T(8,128)(2,1)S(1)}, bf16[1,3,160,256]{3,2,1,0:T(8,128)(2,1)S(1)}, u32[]{:S(2)}, u32[]{:S(2)}) collective-permute-start(bf16[1,3,160,256]{3,2,1,0:T(8,128)(2,1)S(1)} %constant_dynamic-slice_fusion.1), channel_id=1, source_target_pairs={{0,19},{1,18},{2,17},{3,16},{4,23},{5,22},{6,21},{7,20},{8,27},{9,... | collective-permute-start | bytes 737288 | tf_op jit(solution)/shard_map/ppermute | solution.py:451
  14.5 11.9 %shard_map.101 = (bf16[2,512,5376]{2,1,0:T(8,128)(2,1)}, bf16[2,2,256,128]{3,2,1,0:T(8,128)(2,1)}) custom-call(s32[4]{0:T(128)} %pad_add_fusion.5.spot_ref, bf16[16,4,16,3,2,1792]{5,4,3,2,1,0:T(2,128)(2,1)} %bitcast.39), custom_call_target="tpu_custom_call" | custom-call | flops 100000000 | bytes 23000000 | tf_op jit(solution)/shard_map/pallas_call | solution.py:155
  26.4 1.6 collective-permute-start.11
  28.5 1.6 collective-permute-start.12
  30.1 11.8 %shard_map.102 = (bf16[2,512,5376]{2,1,0:T(8,128)(2,1)}, bf16[2,2,256,128]{3,2,1,0:T(8,128)(2,1)}) custom-call(s32[4]{0:T(128)} %pad_add_fusion.5.spot_ref, bf16[16,4,16,3,2,1792]{5,4,3,2,1,0:T(2,128)(2,1)} %bitcast.40), custom_call_target="tpu_custom_call" | custom-call | flops 100000000 | bytes 23000000 | tf_op jit(solution)/shard_map/pallas_call | solution.py:155
  45.0 3.7 %copy.19 = bf16[128,16,1,2,3,64]{0,1,5,4,3,2:T(8,128)(2,1)} copy(bf16[128,16,1,2,3,64]{0,5,4,3,2,1:T(8,128)(2,1)} %param.14) | data formatting | bytes 3145728 | tf_op args[2]
  49.5 3.8 %collective-permute-done.15 = bf16[2,2,256,128]{3,2,1,0:T(8,128)(2,1)S(1)} collective-permute-done((bf16[2,2,256,128]{3,2,1,0:T(8,128)(2,1)}, bf16[2,2,256,128]{3,2,1,0:T(8,128)(2,1)S(1)}, u32[]{:S(2)}, u32[]{:S(2)}) %collective-permute-start.15) | collective-permute-done | bytes 262176 | tf_op jit(solution)/shard_map/ppermute | solution.py:451
  53.2 1.2 pad_maximum_fusion.refs_0_.refs_2_
  54.5 10.1 %shard_map.103 = bf16[5376,1280]{1,0:T(8,128)(2,1)} custom-call(s32[4]{0:T(128)} %pad_add_fusion.5.spot_ref, s32[112]{0:T(128)S(1)} %copy-done.24, bf16[10,3,160,256]{3,2,1,0:T(8,128)(2,1)} %copy-done.4, bf16[10,3,160,256]{3,2,1,0:T(8,128)(2,1)} %collective-permute-done.14.far_ref), custom_call_target="tpu_custom_call" | custom-call | flops 1000000 | bytes 18000000 | tf_op jit(solution)/shard_map/pallas_call | solution.py:112
  66.4 18.0 %shard_map.104 = (f32[2,256,1024]{2,1,0:T(8,128)}, s16[2,2,272,256]{3,2,1,0:T(8,128)(2,1)}, s16[2,272,256]{2,1,0:T(8,128)(2,1)}, s16[2,272,256]{2,1,0:T(8,128)(2,1)}) custom-call(s32[4]{0:T(128)} %pad_add_fusion.5.spot_ref, bf16[2,512,5376]{2,1,0:T(8,128)(2,1)} %get-tuple-element.334.t_ref, bf16[5376,1280]{1,0:T(8,128)(2,1)} %get-tuple-element.341.v_ref, ...), custom_call_target="tpu_custom_call" | custom-call | flops 7200000000 | bytes 24000000 | tf_op jit(solution)/shard_map/pallas_call | solution.py:284
  84.4 7.8 %collective-permute-start.18 = (s16[2,272,256]{2,1,0:T(8,128)(2,1)}, s16[2,272,256]{2,1,0:T(8,128)(2,1)S(1)}, u32[]{:S(2)}, u32[]{:S(2)}) collective-permute-start(s16[2,272,256]{2,1,0:T(8,128)(2,1)} %get-tuple-element.349), channel_id=1, source_target_pairs={{0,13},{1,12},{2,15},{3,14},{4,9},{5,8},{6,11},{7,10},{8,5},{9,4},... | collective-permute-start | bytes 835592 | tf_op jit(solution)/shard_map/ppermute | solution.py:451
  93.2 1.2 collective-permute-start.17
  94.4 17.9 %shard_map.105 = (f32[2,256,1024]{2,1,0:T(8,128)}, s16[2,2,272,256]{3,2,1,0:T(8,128)(2,1)}, s16[2,272,256]{2,1,0:T(8,128)(2,1)}, s16[2,272,256]{2,1,0:T(8,128)(2,1)}) custom-call(s32[4]{0:T(128)} %pad_add_fusion.5.spot_ref, bf16[2,512,5376]{2,1,0:T(8,128)(2,1)} %get-tuple-element.334.t_ref, bf16[5376,1280]{1,0:T(8,128)(2,1)} %get-tuple-element.341.v_ref, ...), custom_call_target="tpu_custom_call" | custom-call | flops 7200000000 | bytes 24000000 | tf_op jit(solution)/shard_map/pallas_call | solution.py:284
  112.3 1.7 collective-permute-start.21
  114.5 3.0 %collective-permute-done.17.refs_0_ = s16[2,2,272,256]{3,2,1,0:T(8,128)(2,1)S(1)} collective-permute-done((s16[2,2,272,256]{3,2,1,0:T(8,128)(2,1)}, s16[2,2,272,256]{3,2,1,0:T(8,128)(2,1)S(1)}, u32[]{:S(2)}, u32[]{:S(2)}) %collective-permute-start.17) | collective-permute-done | bytes 557088 | tf_op jit(solution)/shard_map/ppermute | solution.py:451
  117.6 1.5 collective-permute-start.23
  119.1 18.0 %shard_map.106 = (f32[2,256,1024]{2,1,0:T(8,128)}, s16[2,2,272,256]{3,2,1,0:T(8,128)(2,1)}, s16[2,272,256]{2,1,0:T(8,128)(2,1)}, s16[2,272,256]{2,1,0:T(8,128)(2,1)}) custom-call(s32[4]{0:T(128)} %pad_add_fusion.5.spot_ref, bf16[2,512,5376]{2,1,0:T(8,128)(2,1)} %get-tuple-element.352.t_ref, bf16[5376,1280]{1,0:T(8,128)(2,1)} %get-tuple-element.341.v_ref, ...), custom_call_target="tpu_custom_call" | custom-call | flops 7200000000 | bytes 24000000 | tf_op jit(solution)/shard_map/pallas_call | solution.py:284
  137.2 2.5 %collective-permute-start.25 = (s16[2,272,256]{2,1,0:T(8,128)(2,1)}, s16[2,272,256]{2,1,0:T(8,128)(2,1)S(1)}, u32[]{:S(2)}, u32[]{:S(2)}) collective-permute-start(s16[2,272,256]{2,1,0:T(8,128)(2,1)} %get-tuple-element.367), channel_id=1, source_target_pairs={{0,9},{1,8},{2,11},{3,10},{4,13},{5,12},{6,15},{7,14},{8,1},{9,0},... | collective-permute-start | bytes 835592 | tf_op jit(solution)/shard_map/ppermute | solution.py:451
  139.7 1.5 collective-permute-start.26
  141.9 1.5 collective-permute-start.24
  144.3 7.0 %shard_map.107.refs_4_ = bf16[16,4,16,2,16,64]{5,4,3,2,1,0:T(8,128)(2,1)} custom-call(s32[4]{0:T(128)} %pad_add_fusion.5.spot_ref, f32[128]{0:T(128)} %occ_ref.7, f32[64]{0:T(128)} %vir_ref.7, bf16[256,256]{1,0:T(8,128)(2,1)} %constant.106.clone.turn_ref, bf16[256,256]{1,0:T(8,128)(2,1)} %constant.108.clone.swap_ref, ...), custom_call_target="tpu_custom_call" | custom-call | flops 2000000000 | bytes 10000000 | tf_op jit(solution)/shard_map/pallas_call | solution.py:399
  151.3 18.0 %shard_map.108 = (f32[2,256,1024]{2,1,0:T(8,128)}, s16[2,2,272,256]{3,2,1,0:T(8,128)(2,1)}, s16[2,272,256]{2,1,0:T(8,128)(2,1)}, s16[2,272,256]{2,1,0:T(8,128)(2,1)}) custom-call(s32[4]{0:T(128)} %pad_add_fusion.5.spot_ref, bf16[2,512,5376]{2,1,0:T(8,128)(2,1)} %get-tuple-element.352.t_ref, bf16[5376,1280]{1,0:T(8,128)(2,1)} %get-tuple-element.341.v_ref, ...), custom_call_target="tpu_custom_call" | custom-call | flops 7200000000 | bytes 24000000 | tf_op jit(solution)/shard_map/pallas_call | solution.py:284
  169.4 1.6 collective-permute-start.28
  171.4 1.5 collective-permute-start.32
  173.7 7.0 %shard_map.109.refs_4_ = bf16[16,4,16,2,16,64]{5,4,3,2,1,0:T(8,128)(2,1)} custom-call(s32[4]{0:T(128)} %pad_add_fusion.5.spot_ref, f32[128]{0:T(128)} %occ_ref.7, f32[64]{0:T(128)} %vir_ref.7, bf16[256,256]{1,0:T(8,128)(2,1)} %constant.106.clone.turn_ref, bf16[256,256]{1,0:T(8,128)(2,1)} %constant.108.clone.swap_ref, ...), custom_call_target="tpu_custom_call", output_to_operand_aliasing={{}: (10, {})} | custom-call | flops 2000000000 | bytes 10000000 | tf_op jit(solution)/shard_map/pallas_call | solution.py:399
  181.6 3.5 %collective-permute-done.29.refs_2_ = s16[2,272,256]{2,1,0:T(8,128)(2,1)S(1)} collective-permute-done((s16[2,272,256]{2,1,0:T(8,128)(2,1)}, s16[2,272,256]{2,1,0:T(8,128)(2,1)S(1)}, u32[]{:S(2)}, u32[]{:S(2)}) %collective-permute-start.29) | collective-permute-done | bytes 278560 | tf_op jit(solution)/shard_map/ppermute | solution.py:451
  185.2 1.6 collective-permute-start.31
  187.7 7.0 %shard_map.110.refs_5_ = bf16[16,4,16,2,16,64]{5,4,3,2,1,0:T(8,128)(2,1)} custom-call(s32[4]{0:T(128)} %pad_add_fusion.5.spot_ref, f32[128]{0:T(128)} %occ_ref.7, f32[64]{0:T(128)} %vir_ref.7, bf16[256,256]{1,0:T(8,128)(2,1)} %constant.106.clone.turn_ref, bf16[256,256]{1,0:T(8,128)(2,1)} %constant.108.clone.swap_ref, ...), custom_call_target="tpu_custom_call", output_to_operand_aliasing={{}: (10, {})} | custom-call | flops 2000000000 | bytes 10000000 | tf_op jit(solution)/shard_map/pallas_call | solution.py:399
  194.7 1.4 collective-permute-done.31.refs_4_
  196.8 7.0 %shard_map.111 = bf16[16,4,16,2,16,64]{5,4,3,2,1,0:T(8,128)(2,1)} custom-call(s32[4]{0:T(128)} %pad_add_fusion.5.spot_ref, f32[128]{0:T(128)} %occ_ref.7, f32[64]{0:T(128)} %vir_ref.7, bf16[256,256]{1,0:T(8,128)(2,1)} %constant.106.clone.turn_ref, bf16[256,256]{1,0:T(8,128)(2,1)} %constant.108.clone.swap_ref, ...), custom_call_target="tpu_custom_call", output_to_operand_aliasing={{}: (11, {})} | custom-call | flops 2000000000 | bytes 10000000 | tf_op jit(solution)/shard_map/pallas_call | solution.py:399
  (111 shorter events, 15.7 us)
Async XLA Ops:
  5.2 21.2 %collective-permute-start.7 = (bf16[2,3,160,256]{3,2,1,0:T(8,128)(2,1)}, bf16[2,3,160,256]{3,2,1,0:T(8,128)(2,1)S(1)}, u32[]{:S(2)}, u32[]{:S(2)}) collective-permute-start(bf16[2,3,160,256]{3,2,1,0:T(8,128)(2,1)} %shard_map.100), channel_id=1, source_target_pairs={{0,8},{1,9},{2,10},{3,11},{4,12},{5,13},{6,14},{7,15},{8,0},{9,1},... | collective-permute-start | bytes 1474568 | tf_op jit(solution)/shard_map/ppermute | solution.py:451
  9.2 17.2 %collective-permute-start.9 = (bf16[1,3,160,256]{3,2,1,0:T(8,128)(2,1)S(1)}, bf16[1,3,160,256]{3,2,1,0:T(8,128)(2,1)S(1)}, u32[]{:S(2)}, u32[]{:S(2)}) collective-permute-start(bf16[1,3,160,256]{3,2,1,0:T(8,128)(2,1)S(1)} %constant_dynamic-slice_fusion.1), channel_id=1, source_target_pairs={{0,19},{1,18},{2,17},{3,16},{4,23},{5,22},{6,21},{7,20},{8,27},{9,... | collective-permute-start | bytes 737288 | tf_op jit(solution)/shard_map/ppermute | solution.py:451
  13.7 12.7 %collective-permute-start.8 = (bf16[1,3,160,256]{3,2,1,0:T(8,128)(2,1)S(1)}, bf16[1,3,160,256]{3,2,1,0:T(8,128)(2,1)S(1)}, u32[]{:S(2)}, u32[]{:S(2)}) collective-permute-start(bf16[1,3,160,256]{3,2,1,0:T(8,128)(2,1)S(1)} %constant_dynamic-slice_fusion.1), channel_id=1, source_target_pairs={{0,3},{1,2},{2,1},{3,0},{4,7},{5,6},{6,5},{7,4},{8,11},{9,10},{10,... | collective-permute-start | bytes 737288 | tf_op jit(solution)/shard_map/ppermute | solution.py:451
  14.0 27.9 %collective-permute-start.10 = (bf16[2,3,160,256]{3,2,1,0:T(8,128)(2,1)}, bf16[2,3,160,256]{3,2,1,0:T(8,128)(2,1)}, u32[]{:S(2)}, u32[]{:S(2)}) collective-permute-start(bf16[2,3,160,256]{3,2,1,0:T(8,128)(2,1)} %shard_map.100), channel_id=1, source_target_pairs={{0,16},{1,17},{2,18},{3,19},{4,20},{5,21},{6,22},{7,23},{8,24},{9,... | collective-permute-start | bytes 1474568 | tf_op jit(solution)/shard_map/ppermute | solution.py:451
  14.5 15.6 %copy-start.5 = (bf16[2,3,160,256]{3,2,1,0:T(8,128)(2,1)S(1)}, bf16[2,3,160,256]{3,2,1,0:T(8,128)(2,1)}, u32[]{:S(2)}) copy-start(bf16[2,3,160,256]{3,2,1,0:T(8,128)(2,1)} %shard_map.100) | copy-start | bytes 1474564
  26.4 15.5 %collective-permute-start.11 = (bf16[2,3,160,256]{3,2,1,0:T(8,128)(2,1)S(1)}, bf16[2,3,160,256]{3,2,1,0:T(8,128)(2,1)}, u32[]{:S(2)}, u32[]{:S(2)}) collective-permute-start(bf16[2,3,160,256]{3,2,1,0:T(8,128)(2,1)S(1)} %collective-permute-done.7), channel_id=1, source_target_pairs={{0,16},{1,17},{2,18},{3,19},{4,20},{5,21},{6,22},{7,23},{8,24},{9,... | collective-permute-start | bytes 1474568 | tf_op jit(solution)/shard_map/ppermute | solution.py:451
  28.0 13.9 %collective-permute-start.13 = (bf16[2,2,256,128]{3,2,1,0:T(8,128)(2,1)}, bf16[2,2,256,128]{3,2,1,0:T(8,128)(2,1)}, u32[]{:S(2)}, u32[]{:S(2)}) collective-permute-start(bf16[2,2,256,128]{3,2,1,0:T(8,128)(2,1)} %get-tuple-element.324), channel_id=1, source_target_pairs={{0,8},{1,9},{2,10},{3,11},{4,12},{5,13},{6,14},{7,15},{8,0},{9,1},... | collective-permute-start | bytes 786440 | tf_op jit(solution)/shard_map/ppermute | solution.py:451
  28.5 13.4 %collective-permute-start.12 = (bf16[1,3,160,256]{3,2,1,0:T(8,128)(2,1)S(1)}, bf16[1,3,160,256]{3,2,1,0:T(8,128)(2,1)S(1)}, u32[]{:S(2)}, u32[]{:S(2)}) collective-permute-start(bf16[1,3,160,256]{3,2,1,0:T(8,128)(2,1)S(1)} %broadcast_select_fusion.1), channel_id=1, source_target_pairs={{0,8},{1,9},{2,10},{3,11},{4,12},{5,13},{6,14},{7,15},{8,0},{9,1},... | collective-permute-start | bytes 737288 | tf_op jit(solution)/shard_map/ppermute | solution.py:451
  44.2 9.0 %collective-permute-start.14 = (bf16[10,3,160,256]{3,2,1,0:T(8,128)(2,1)S(1)}, bf16[10,3,160,256]{3,2,1,0:T(8,128)(2,1)}, u32[]{:S(2)}, u32[]{:S(2)}) collective-permute-start(bf16[10,3,160,256]{3,2,1,0:T(8,128)(2,1)S(1)} %constant_dynamic-update-slice_fusion.6.near_ref), channel_id=1, source_target_pairs={{0,4},{1,5},{2,6},{3,7},{4,0},{5,1},{6,2},{7,3},{8,12},{9,13},{10,... | collective-permute-start | bytes 7372808 | tf_op jit(solution)/shard_map/ppermute | solution.py:451
  44.3 8.9 %collective-permute-start.15 = (bf16[2,2,256,128]{3,2,1,0:T(8,128)(2,1)}, bf16[2,2,256,128]{3,2,1,0:T(8,128)(2,1)S(1)}, u32[]{:S(2)}, u32[]{:S(2)}) collective-permute-start(bf16[2,2,256,128]{3,2,1,0:T(8,128)(2,1)} %get-tuple-element.332), channel_id=1, source_target_pairs={{0,8},{1,9},{2,10},{3,11},{4,12},{5,13},{6,14},{7,15},{8,0},{9,1},... | collective-permute-start | bytes 786440 | tf_op jit(solution)/shard_map/ppermute | solution.py:451
  54.4 10.2 %collective-permute-start.16 = (bf16[4,2,2,256,128]{4,3,2,1,0:T(8,128)(2,1)S(1)}, bf16[4,2,2,256,128]{4,3,2,1,0:T(8,128)(2,1)S(1)}, u32[]{:S(2)}, u32[]{:S(2)}) collective-permute-start(bf16[4,2,2,256,128]{4,3,2,1,0:T(8,128)(2,1)S(1)} %pad_maximum_fusion.refs_0_.refs_2_), channel_id=1, source_target_pairs={{0,4},{1,5},{2,6},{3,7},{4,0},{5,1},{6,2},{7,3},{8,12},{9,13},{10,... | collective-permute-start | bytes 3145736 | tf_op jit(solution)/shard_map/ppermute | solution.py:451
  84.4 29.6 %collective-permute-start.18 = (s16[2,272,256]{2,1,0:T(8,128)(2,1)}, s16[2,272,256]{2,1,0:T(8,128)(2,1)S(1)}, u32[]{:S(2)}, u32[]{:S(2)}) collective-permute-start(s16[2,272,256]{2,1,0:T(8,128)(2,1)} %get-tuple-element.349), channel_id=1, source_target_pairs={{0,13},{1,12},{2,15},{3,14},{4,9},{5,8},{6,11},{7,10},{8,5},{9,4},... | collective-permute-start | bytes 835592 | tf_op jit(solution)/shard_map/ppermute | solution.py:451
  92.2 22.3 %collective-permute-start.19 = (s16[2,272,256]{2,1,0:T(8,128)(2,1)}, s16[2,272,256]{2,1,0:T(8,128)(2,1)S(1)}, u32[]{:S(2)}, u32[]{:S(2)}) collective-permute-start(s16[2,272,256]{2,1,0:T(8,128)(2,1)} %get-tuple-element.350), channel_id=1, source_target_pairs={{0,14},{1,15},{2,12},{3,13},{4,10},{5,11},{6,8},{7,9},{8,6},{9,7},... | collective-permute-start | bytes 835592 | tf_op jit(solution)/shard_map/ppermute | solution.py:451
  93.2 24.2 %collective-permute-start.17 = (s16[2,2,272,256]{3,2,1,0:T(8,128)(2,1)}, s16[2,2,272,256]{3,2,1,0:T(8,128)(2,1)S(1)}, u32[]{:S(2)}, u32[]{:S(2)}) collective-permute-start(s16[2,2,272,256]{3,2,1,0:T(8,128)(2,1)} %get-tuple-element.348), channel_id=1, source_target_pairs={{0,12},{1,13},{2,14},{3,15},{4,8},{5,9},{6,10},{7,11},{8,4},{9,5},... | collective-permute-start | bytes 1671176 | tf_op jit(solution)/shard_map/ppermute | solution.py:451
  112.3 24.8 %collective-permute-start.21 = (s16[2,272,256]{2,1,0:T(8,128)(2,1)}, s16[2,272,256]{2,1,0:T(8,128)(2,1)S(1)}, u32[]{:S(2)}, u32[]{:S(2)}) collective-permute-start(s16[2,272,256]{2,1,0:T(8,128)(2,1)} %get-tuple-element.356), channel_id=1, source_target_pairs={{0,5},{1,4},{2,7},{3,6},{4,1},{5,0},{6,3},{7,2},{8,13},{9,12},{10,... | collective-permute-start | bytes 835592 | tf_op jit(solution)/shard_map/ppermute | solution.py:451
  113.9 23.2 %collective-permute-start.22 = (s16[2,272,256]{2,1,0:T(8,128)(2,1)}, s16[2,272,256]{2,1,0:T(8,128)(2,1)S(1)}, u32[]{:S(2)}, u32[]{:S(2)}) collective-permute-start(s16[2,272,256]{2,1,0:T(8,128)(2,1)} %get-tuple-element.357), channel_id=1, source_target_pairs={{0,6},{1,7},{2,4},{3,5},{4,2},{5,3},{6,0},{7,1},{8,14},{9,15},{10,... | collective-permute-start | bytes 835592 | tf_op jit(solution)/shard_map/ppermute | solution.py:451
  114.0 23.1 %copy-start.16 = (s16[2,272,256]{2,1,0:T(8,128)(2,1)}, s16[2,272,256]{2,1,0:T(8,128)(2,1)S(1)}, u32[]{:S(2)}) copy-start(s16[2,272,256]{2,1,0:T(8,128)(2,1)S(1)} %collective-permute-done.18.refs_1_) | copy-start | bytes 835588
  114.0 23.1 %collective-permute-start.20 = (s16[2,2,272,256]{3,2,1,0:T(8,128)(2,1)}, s16[2,2,272,256]{3,2,1,0:T(8,128)(2,1)S(1)}, u32[]{:S(2)}, u32[]{:S(2)}) collective-permute-start(s16[2,2,272,256]{3,2,1,0:T(8,128)(2,1)} %get-tuple-element.355), channel_id=1, source_target_pairs={{0,4},{1,5},{2,6},{3,7},{4,0},{5,1},{6,2},{7,3},{8,12},{9,13},{10,... | collective-permute-start | bytes 1671176 | tf_op jit(solution)/shard_map/ppermute | solution.py:451
  114.5 22.6 %copy-start.17 = (s16[2,272,256]{2,1,0:T(8,128)(2,1)}, s16[2,272,256]{2,1,0:T(8,128)(2,1)S(1)}, u32[]{:S(2)}) copy-start(s16[2,272,256]{2,1,0:T(8,128)(2,1)S(1)} %collective-permute-done.19.refs_2_) | copy-start | bytes 835588
  117.5 19.6 %copy-start.9 = (s16[2,2,272,256]{3,2,1,0:T(8,128)(2,1)}, s16[2,2,272,256]{3,2,1,0:T(8,128)(2,1)S(1)}, u32[]{:S(2)}) copy-start(s16[2,2,272,256]{3,2,1,0:T(8,128)(2,1)S(1)} %collective-permute-done.17.refs_0_) | copy-start | bytes 1671172
  117.6 25.9 %collective-permute-start.23 = (s16[4,272,256]{2,1,0:T(8,128)(2,1)S(1)}, s16[4,272,256]{2,1,0:T(8,128)(2,1)S(1)}, u32[]{:S(2)}, u32[]{:S(2)}) collective-permute-start(s16[4,272,256]{2,1,0:T(8,128)(2,1)S(1)} %pad_add_fusion.1), channel_id=1, source_target_pairs={{0,16},{1,17},{2,18},{3,19},{4,20},{5,21},{6,22},{7,23},{8,24},{9,... | collective-permute-start | bytes 1671176 | tf_op jit(solution)/shard_map/ppermute | solution.py:451
  137.1 14.2 %copy-start.10 = (s16[2,272,256]{2,1,0:T(8,128)(2,1)}, s16[2,272,256]{2,1,0:T(8,128)(2,1)S(1)}, u32[]{:S(2)}) copy-start(s16[2,272,256]{2,1,0:T(8,128)(2,1)S(1)} %collective-permute-done.21.refs_1_) | copy-start | bytes 835588
  137.1 14.2 %copy-start.11 = (s16[2,272,256]{2,1,0:T(8,128)(2,1)}, s16[2,272,256]{2,1,0:T(8,128)(2,1)S(1)}, u32[]{:S(2)}) copy-start(s16[2,272,256]{2,1,0:T(8,128)(2,1)S(1)} %collective-permute-done.22.refs_2_) | copy-start | bytes 835588
  137.2 32.1 %collective-permute-start.25 = (s16[2,272,256]{2,1,0:T(8,128)(2,1)}, s16[2,272,256]{2,1,0:T(8,128)(2,1)S(1)}, u32[]{:S(2)}, u32[]{:S(2)}) collective-permute-start(s16[2,272,256]{2,1,0:T(8,128)(2,1)} %get-tuple-element.367), channel_id=1, source_target_pairs={{0,9},{1,8},{2,11},{3,10},{4,13},{5,12},{6,15},{7,14},{8,1},{9,0},... | collective-permute-start | bytes 835592 | tf_op jit(solution)/shard_map/ppermute | solution.py:451
  139.7 29.5 %collective-permute-start.26 = (s16[2,272,256]{2,1,0:T(8,128)(2,1)}, s16[2,272,256]{2,1,0:T(8,128)(2,1)S(1)}, u32[]{:S(2)}, u32[]{:S(2)}) collective-permute-start(s16[2,272,256]{2,1,0:T(8,128)(2,1)} %get-tuple-element.368), channel_id=1, source_target_pairs={{0,10},{1,11},{2,8},{3,9},{4,14},{5,15},{6,12},{7,13},{8,2},{9,3},... | collective-permute-start | bytes 835592 | tf_op jit(solution)/shard_map/ppermute | solution.py:451
  141.3 31.6 %collective-permute-start.27 = (s16[4,272,256]{2,1,0:T(8,128)(2,1)S(1)}, s16[4,272,256]{2,1,0:T(8,128)(2,1)S(1)}, u32[]{:S(2)}, u32[]{:S(2)}) collective-permute-start(s16[4,272,256]{2,1,0:T(8,128)(2,1)S(1)} %pad_add_fusion.2), channel_id=1, source_target_pairs={{0,16},{1,17},{2,18},{3,19},{4,20},{5,21},{6,22},{7,23},{8,24},{9,... | collective-permute-start | bytes 1671176 | tf_op jit(solution)/shard_map/ppermute | solution.py:451
  141.9 27.4 %collective-permute-start.24 = (s16[2,2,272,256]{3,2,1,0:T(8,128)(2,1)}, s16[2,2,272,256]{3,2,1,0:T(8,128)(2,1)S(1)}, u32[]{:S(2)}, u32[]{:S(2)}) collective-permute-start(s16[2,2,272,256]{3,2,1,0:T(8,128)(2,1)} %get-tuple-element.366), channel_id=1, source_target_pairs={{0,8},{1,9},{2,10},{3,11},{4,12},{5,13},{6,14},{7,15},{8,0},{9,1},... | collective-permute-start | bytes 1671176 | tf_op jit(solution)/shard_map/ppermute | solution.py:451
  169.4 12.3 %collective-permute-start.28 = (s16[2,272,256]{2,1,0:T(8,128)(2,1)}, s16[2,272,256]{2,1,0:T(8,128)(2,1)S(1)}, u32[]{:S(2)}, u32[]{:S(2)}) collective-permute-start(s16[2,272,256]{2,1,0:T(8,128)(2,1)} %get-tuple-element.376), channel_id=1, source_target_pairs={{0,1},{1,0},{2,3},{3,2},{4,5},{5,4},{6,7},{7,6},{8,9},{9,8},{10,11... | collective-permute-start | bytes 835592 | tf_op jit(solution)/shard_map/ppermute | solution.py:451
  170.9 14.2 %collective-permute-start.29 = (s16[2,272,256]{2,1,0:T(8,128)(2,1)}, s16[2,272,256]{2,1,0:T(8,128)(2,1)S(1)}, u32[]{:S(2)}, u32[]{:S(2)}) collective-permute-start(s16[2,272,256]{2,1,0:T(8,128)(2,1)} %get-tuple-element.377), channel_id=1, source_target_pairs={{0,2},{1,3},{2,0},{3,1},{4,6},{5,7},{6,4},{7,5},{8,10},{9,11},{10,... | collective-permute-start | bytes 835592 | tf_op jit(solution)/shard_map/ppermute | solution.py:451
  171.4 15.5 %collective-permute-start.32 = (s16[4,272,256]{2,1,0:T(8,128)(2,1)S(1)}, s16[4,272,256]{2,1,0:T(8,128)(2,1)S(1)}, u32[]{:S(2)}, u32[]{:S(2)}) collective-permute-start(s16[4,272,256]{2,1,0:T(8,128)(2,1)S(1)} %pad_add_fusion.3), channel_id=1, source_target_pairs={{0,16},{1,17},{2,18},{3,19},{4,20},{5,21},{6,22},{7,23},{8,24},{9,... | collective-permute-start | bytes 1671176 | tf_op jit(solution)/shard_map/ppermute | solution.py:451
  180.8 13.9 %collective-permute-start.30 = (s16[2,272,256]{2,1,0:T(8,128)(2,1)S(1)}, s16[2,272,256]{2,1,0:T(8,128)(2,1)S(1)}, u32[]{:S(2)}, u32[]{:S(2)}) collective-permute-start(s16[2,272,256]{2,1,0:T(8,128)(2,1)S(1)} %slice_bitcast_fusion.1), channel_id=1, source_target_pairs={{0,16},{1,17},{2,18},{3,19},{4,20},{5,21},{6,22},{7,23},{8,24},{9,... | collective-permute-start | bytes 835592 | tf_op jit(solution)/shard_map/ppermute | solution.py:451
  185.2 10.9 %collective-permute-start.31 = (s16[2,272,256]{2,1,0:T(8,128)(2,1)S(1)}, s16[2,272,256]{2,1,0:T(8,128)(2,1)S(1)}, u32[]{:S(2)}, u32[]{:S(2)}) collective-permute-start(s16[2,272,256]{2,1,0:T(8,128)(2,1)S(1)} %pad_add_fusion.4), channel_id=1, source_target_pairs={{0,16},{1,17},{2,18},{3,19},{4,20},{5,21},{6,22},{7,23},{8,24},{9,... | collective-permute-start | bytes 835592 | tf_op jit(solution)/shard_map/ppermute | solution.py:451
  (18 other events, 128.6 us)
